TPU v7x, 256 devices: a whole 4x4x8 slice. The times are simulated.
256 devices in a mesh: replica: 8 (over y, core), fsdp: 32 (over x, z).
Axes of the slice: x: 4, y: 4, z: 8, core: 2. Of those that a mesh axis runs over, the one named last changes fastest.
Arguments:
- gradients: bfloat16 [8, 4096, 8192], P('replica', 'fsdp'), may hold values from -6 to 6
- left_factor: float32 [32, 1, 8, 512, 512], P('fsdp', None, None, 'replica'), may hold values from -6 to 6
- right_factor: float32 [32, 1, 8, 512, 512], P('fsdp', None, None, 'replica'), may hold values from -6 to 6
- left_root: bfloat16 [32, 1, 8, 512, 512], P('fsdp', None, None, 'replica'), may hold values from -0.25 to 0.25
- right_root: bfloat16 [32, 1, 8, 512, 512], P('fsdp'), may hold values from -0.25 to 0.25
- owner_table: int32 [8, 16], replicated, may hold values from 0 to 31, as said below
Outputs:
- left_next: float32 [32, 1, 8, 512, 512], P('fsdp', None, None, 'replica')
- right_next: float32 [32, 1, 8, 512, 512], P('fsdp', None, None, 'replica')
- update: bfloat16 [32, 1, 8, 512, 512], P('fsdp', None, None, 'replica')
Inputs may be any that keep to these rules, and one draw needn't show every extreme that they name: In each row of owner_table no owner is named more than 1 times.
All inputs are finite; a program needn't handle non-finite values.
Results may differ from a plain program's by a relative error of at most 0.02.
Values may be sent and summed in bfloat16 or wider, within the bound.
No kernel may reach another device: no remote copies, remote signals or barrier semaphores. Data moves between devices by JAX's collectives and lax.ppermute only.
A program may use at most 64 MiB of HBM per device.

v0:
```python
import jax
import jax.numpy as jnp
from jax import lax
from jax.sharding import PartitionSpec as P

decay_rate = 0.9


def slot_table(owner_table, owner_count, slot_depth):
    block_cols = owner_table.shape[1]
    owner_match = (
        owner_table[:, :, None] == jnp.arange(owner_count, dtype=jnp.int32)[None, None, :]
    ).astype(jnp.int32)
    earlier = jnp.cumsum(owner_match, axis=1) - owner_match
    column_rank = jnp.sum(earlier * owner_match, axis=2)
    slot_match = (
        column_rank[:, :, None] == jnp.arange(slot_depth, dtype=jnp.int32)[None, None, :]
    ).astype(jnp.int32)
    joint = owner_match[:, :, None, :] * slot_match[:, :, :, None]
    column_ids = jnp.arange(block_cols, dtype=jnp.int32)[None, :, None, None]
    col_table = jnp.sum(joint * column_ids, axis=1)
    col_valid = jnp.sum(joint, axis=1)
    return (col_table, col_valid)


def shards(gradients, left_factor, right_factor, left_root, right_root, owner_table):
    local = gradients[0].astype(jnp.float32)
    row_count, col_count = local.shape
    fsdp_count = lax.axis_size("fsdp")
    block_size = left_factor.shape[-1]
    slot_depth = left_factor.shape[1]
    block_rows = left_factor.shape[2]
    share_rows = left_factor.shape[3]
    block_cols = col_count // block_size
    per_block = block_size // row_count
    summed = lax.psum(local.astype(jnp.bfloat16), "replica")
    col_table, col_valid = slot_table(owner_table, fsdp_count, slot_depth)
    owner_index = lax.axis_index("fsdp")
    replica_index = lax.axis_index("replica")
    my_row = owner_index // per_block
    column_pick = lax.dynamic_index_in_dim(col_table, my_row, 0, keepdims=False)
    slot_live = lax.dynamic_index_in_dim(col_valid, my_row, 0, keepdims=False)
    strip_rows = summed.shape[0]
    strips = jnp.transpose(summed.reshape(strip_rows, block_cols, block_size), (1, 0, 2))
    outgoing = jnp.take(strips, column_pick.reshape(-1), axis=0)
    outgoing = outgoing.reshape(slot_depth, fsdp_count, strip_rows, block_size)
    outgoing = outgoing * slot_live[:, :, None, None].astype(jnp.bfloat16)
    received = lax.all_to_all(outgoing, "fsdp", split_axis=1, concat_axis=1, tiled=True)
    whole_blocks = received.reshape(slot_depth, block_rows, block_size, block_size)
    scale = (1.0 - decay_rate) / block_size
    left_mine = left_factor[0]
    right_mine = right_factor[0]
    lroot_mine = left_root[0]
    rroot_mine = right_root[0]
    offset = replica_index * share_rows
    row_share = lax.dynamic_slice_in_dim(whole_blocks, offset, share_rows, 2)
    col_share = lax.dynamic_slice_in_dim(whole_blocks, offset, share_rows, 3)
    stat_left = jnp.einsum(
        "kjab,kjcb->kjac", row_share, whole_blocks, preferred_element_type=jnp.float32
    )
    stat_right = jnp.einsum(
        "kjba,kjbc->kjac", col_share, whole_blocks, preferred_element_type=jnp.float32
    )
    left_new = decay_rate * left_mine + scale * stat_left
    right_new = decay_rate * right_mine + scale * stat_right
    half = jnp.einsum(
        "kjab,kjbc->kjac", lroot_mine, whole_blocks, preferred_element_type=jnp.float32
    ).astype(jnp.bfloat16)
    result = jnp.einsum(
        "kjab,kjbc->kjac", half, rroot_mine, preferred_element_type=jnp.float32
    ).astype(jnp.bfloat16)
    return (left_new[None], right_new[None], result[None])


def solution(mesh):
    placed = (
        P("replica", "fsdp", None),
        P("fsdp", None, None, "replica", None),
        P("fsdp", None, None, "replica", None),
        P("fsdp", None, None, "replica", None),
        P("fsdp", None, None, None, None),
        P(),
    )
    return jax.shard_map(
        shards,
        mesh=mesh,
        in_specs=placed,
        out_specs=(
            P("fsdp", None, None, "replica", None),
            P("fsdp", None, None, "replica", None),
            P("fsdp", None, None, "replica", None),
        ),
        check_vma=False,
    )
```

profile of v0, /device:TPU:123, one launch (start us, length us, event | category | flops | bytes accessed | tf_op | source)
XLA Modules:
  0.0 225.1 jit_solution(10695324094805372945)
XLA Ops:
  7.2 0.0 copy-start
  7.2 0.0 all-reduce.2.cloned.1.call-start
  7.2 3.3 %copy.31 = bf16[1,128,8192]{1,2,0:T(8,128)(2,1)S(1)} copy(bf16[1,128,8192]{2,1,0:T(8,128)(2,1)} %param.6) | data formatting | bytes 4194304 | tf_op args[0]
  10.5 0.0 copy-start.3
  10.5 2.6 %copy.32 = bf16[128,16,512]{2,0,1:T(8,128)(2,1)} copy(bf16[128,16,512]{0,2,1:T(8,128)(2,1)S(1)} %bitcast.52) | data formatting | bytes 4194304 | tf_op jit(solution)/shard_map/reshape | solution.py:44
  13.2 0.0 all-reduce.2.cloned.1.call-update
  13.2 0.0 copy-done.3
  13.2 0.1 copy.29
  13.3 0.4 fusion.29
  13.7 0.1 copy.30
  13.8 0.1 select_reduce_fusion
  14.0 70.9 %all-reduce.2.cloned.1.call-done = bf16[16,128,512]{2,1,0:T(8,128)(2,1)} async-done(((bf16[16,128,512]{2,1,0:T(8,128)(2,1)}), bf16[16,128,512]{2,1,0:T(8,128)(2,1)}) %all-reduce.2.cloned.1.call-update) | async-done | bytes 2097168 | tf_op jit(solution)/shard_map/psum | solution.py:36
  84.9 4.4 %gather_fusion = bf16[32,128,512]{2,1,0:T(8,128)(2,1)} fusion(bf16[16,128,512]{2,1,0:T(8,128)(2,1)} %all-reduce.2.cloned.1.call-done, s32[1024]{0:T(1024)S(1)} %pad_clamp_fusion), kind=kCustom, calls=%fused_computation | custom fusion | bytes 8388736 | tf_op jit(solution)/shard_map/jit(_take)/gather | solution.py:45
  89.2 4.6 %fusion.3 = bf16[1,32,128,512]{3,2,0,1:T(8,128)(2,1)} fusion(bf16[32,128,512]{2,1,0:T(8,128)(2,1)} %gather_fusion, pred[32]{0:T(512)(128)(4,1)S(1)} %compare_and_fusion, bf16[32]{0:T(256)(128)(2,1)S(1)} %fusion.27), kind=kLoop, calls=%fused_computation.5 | loop fusion | flops 4194304 | bytes 8388704 | tf_op jit(solution)/shard_map/mul | solution.py:47
  93.8 0.0 copy-start.2
  93.9 9.5 %all-to-all-start = ((bf16[1,32,128,512]{3,2,0,1:T(8,128)(2,1)}), bf16[1,32,128,512]{3,2,0,1:T(8,128)(2,1)}, u32[]{:S(2)}, u32[]{:S(2)}) async-start(bf16[1,32,128,512]{3,2,0,1:T(8,128)(2,1)} %fusion.3), calls=%async_computation | async-start | bytes 8388608 | tf_op jit(solution)/shard_map/all_to_all | solution.py:48
  103.4 0.0 copy-start.1
  103.4 99.7 %all-to-all-done = bf16[1,32,128,512]{3,2,0,1:T(8,128)(2,1)} async-done(((bf16[1,32,128,512]{3,2,0,1:T(8,128)(2,1)}), bf16[1,32,128,512]{3,2,0,1:T(8,128)(2,1)}, u32[]{:S(2)}, u32[]{:S(2)}) %all-to-all-start) | async-done | bytes 4194336 | tf_op jit(solution)/shard_map/all_to_all | solution.py:48
  203.1 0.0 copy-done.2
  203.1 4.7 %fusion.5 = f32[1,1,8,64,512]{4,3,2,1,0:T(8,128)} fusion(bf16[8,512,512]{2,1,0:T(8,128)(2,1)} %bitcast.11, bf16[1,8,512,512]{3,2,1,0:T(8,128)(2,1)} %bitcast.9, s32[]{:T(128)S(6)} %select_n.46, f32[1,1,8,64,512]{4,3,2,1,0:T(8,128)S(1)} %copy-done.2), kind=kOutput, calls=%fused_computation.8 | convolution fusion | flops 269221888 | bytes 7340036 | tf_op jit(solution)/shard_map/kjba,kjbc->kjac/dot_general | solution.py:61
  207.7 0.0 copy-done.1
  207.7 4.7 %fusion.7 = f32[1,1,8,64,512]{4,3,2,1,0:T(8,128)} fusion(bf16[8,512,512]{2,1,0:T(8,128)(2,1)} %bitcast.11, f32[1,1,8,64,512]{4,3,2,1,0:T(8,128)S(1)} %copy-done.1, bf16[1,8,512,512]{3,2,1,0:T(8,128)(2,1)} %bitcast.9, s32[]{:T(128)S(6)} %select_n.46), kind=kOutput, calls=%fused_computation.11 | convolution fusion | flops 269221888 | bytes 6815748 | tf_op jit(solution)/shard_map/kjab,kjcb->kjac/dot_general | solution.py:58
  212.5 0.0 copy-done
  212.5 5.8 %fusion.11 = bf16[1,1,8,64,512]{4,3,2,1,0:T(8,128)(2,1)} fusion(bf16[1,1,8,512,512]{4,3,2,1,0:T(8,128)(2,1)} %param.10, bf16[8,512,512]{2,1,0:T(8,128)(2,1)} %bitcast.11, bf16[1,1,8,64,512]{4,3,2,1,0:T(8,128)(2,1)S(1)} %copy-done), kind=kOutput, calls=%fused_computation.14 | convolution fusion | flops 537395200 | bytes 9437184 | tf_op jit(solution)/shard_map/kjab,kjbc->kjac/dot_general | solution.py:69
  (5 shorter events, 0.1 us)
Async XLA Ops:
  7.2 205.3 %copy-start = (bf16[1,1,8,64,512]{4,3,2,1,0:T(8,128)(2,1)S(1)}, bf16[1,1,8,64,512]{4,3,2,1,0:T(8,128)(2,1)}, u32[]{:S(2)}) copy-start(bf16[1,1,8,64,512]{4,3,2,1,0:T(8,128)(2,1)} %param.9) | copy-start | bytes 1572868
  7.2 77.7 %all-reduce.2.cloned.1.call-start = ((), (), s32[]{:S(2)}) async-start(), calls=%async_computation.1 | async-start | bytes 4194304 | tf_op jit(solution)/shard_map/psum | solution.py:36
  10.5 2.7 %copy-start.3 = (s32[8,16]{1,0:T(8,128)S(1)}, s32[8,16]{1,0:T(8,128)}, u32[]{:S(2)}) copy-start(s32[8,16]{1,0:T(8,128)} %param.11) | copy-start | bytes 1540
  93.8 109.2 %copy-start.2 = (f32[1,1,8,64,512]{4,3,2,1,0:T(8,128)S(1)}, f32[1,1,8,64,512]{4,3,2,1,0:T(8,128)}, u32[]{:S(2)}) copy-start(f32[1,1,8,64,512]{4,3,2,1,0:T(8,128)} %param.8) | copy-start | bytes 3145732
  93.9 109.2 %all-to-all-start = ((bf16[1,32,128,512]{3,2,0,1:T(8,128)(2,1)}), bf16[1,32,128,512]{3,2,0,1:T(8,128)(2,1)}, u32[]{:S(2)}, u32[]{:S(2)}) async-start(bf16[1,32,128,512]{3,2,0,1:T(8,128)(2,1)} %fusion.3), calls=%async_computation | async-start | bytes 8388608 | tf_op jit(solution)/shard_map/all_to_all | solution.py:48
  103.4 104.4 %copy-start.1 = (f32[1,1,8,64,512]{4,3,2,1,0:T(8,128)S(1)}, f32[1,1,8,64,512]{4,3,2,1,0:T(8,128)}, u32[]{:S(2)}) copy-start(f32[1,1,8,64,512]{4,3,2,1,0:T(8,128)} %param.7) | copy-start | bytes 3145732
Sparse Core Ops, SparseCore 0:
  13.3 71.5 all-reduce.1
where the time goes:
time: 225 us
  waiting for transfers between devices  171 us (76%)
  matrix products  15.1 us (7%)
  between operations  14.1 us (6%)
  local copies, waits for them, and re-layouts  10.5 us (5%)
  starting transfers between devices  9.53 us (4%)
  other arithmetic  5.2 us (2%)
    all_to_all x1, waiting for transfers between devices, shards(): lax.all_to_all(outgoing, 'fsdp', split_axis=1, concat_axis=1, tiled=True)  99.7 us
    psum x1, waiting for transfers between devices, shards(): summed = lax.psum(local.astype(jnp.bfloat16), 'replica')  70.9 us
    all_to_all x1, starting transfers between devices, shards(): lax.all_to_all(outgoing, 'fsdp', split_axis=1, concat_axis=1, tiled=True)  9.49 us
    dot_general x1, matrix products, shards(): jnp.einsum('kjab,kjbc->kjac', half, rroot_mine, preferred_element_type=jn...  5.77 us
    dot_general x1, matrix products, shards(): jnp.einsum('kjab,kjcb->kjac', row_share, whole_blocks, preferred_element_...  4.71 us
    dot_general x1, matrix products, shards(): jnp.einsum('kjba,kjbc->kjac', col_share, whole_blocks, preferred_element_...  4.66 us
    mul x1, other arithmetic, shards(): outgoing = outgoing * slot_live[:, :, None, None].astype(jnp.bfloat16)  4.61 us
  transfers between devices with their start and end apart: 2, of which 2 were waited for; matrix products, arithmetic and copies ran while one was open for 0% of the time, Pallas kernels for 0%

commit v1 on v0

v1 whole, which is shorter than its diff:
```python
import functools

import jax
import jax.numpy as jnp
from jax import lax
from jax.experimental import pallas as pl
from jax.experimental.pallas import tpu as pltpu
from jax.sharding import PartitionSpec as P

decay_rate = 0.9
MIB = 1 << 20


def y_shift(d):
    return [(r, (r + 2 * d) % 8) for r in range(8)]


core_swap = [(r, r ^ 1) for r in range(8)]


def permute(x, pairs):
    return lax.ppermute(x, "replica", pairs)


def pair_sum_kernel(idx, *refs):
    mine, other, outs = refs[:4], refs[4:8], refs[8:]
    for a, b, o in zip(mine, other, outs):
        o[...] = (a[0].astype(jnp.float32) + b[0].astype(jnp.float32)).astype(o.dtype)


def pair_sum(idx, own, recv):
    groups, rows, cols = own.shape
    step = cols // 4

    def pick(k):
        return lambda t, s: (2 * lax.rem(s[0] // 2 + k, 4) + lax.rem(s[0], 2), 0, t)

    specs = [pl.BlockSpec((1, rows, step), pick(k)) for k in range(4)]
    return pl.pallas_call(
        pair_sum_kernel,
        grid_spec=pltpu.PrefetchScalarGridSpec(
            num_scalar_prefetch=1,
            grid=(cols // step,),
            in_specs=specs + specs,
            out_specs=[pl.BlockSpec((rows, step), lambda t, s: (0, t))] * 4,
        ),
        out_shape=[jax.ShapeDtypeStruct((rows, cols), own.dtype)] * 4,
        compiler_params=pltpu.CompilerParams(vmem_limit_bytes=16 * MIB),
        cost_estimate=pl.CostEstimate(flops=rows * cols * 4, bytes_accessed=24 * rows * cols, transcendentals=0),
        name="pair_sum",
    )(idx, *([own] * 4), *([recv] * 4))


def place_kernel(idx, table, a, b, c, d, out):
    block = out.shape[-1]
    my_row = idx[1] // 4
    out[...] = jnp.zeros_like(out)
    for col in range(a.shape[-1] // block):
        cut = slice(col * block, (col + 1) * block)
        total = (
            a[:, cut].astype(jnp.float32)
            + b[:, cut].astype(jnp.float32)
            + c[:, cut].astype(jnp.float32)
            + d[:, cut].astype(jnp.float32)
        )
        out[table[my_row, col]] = total.astype(out.dtype)


def place(idx, table, parts, owners, block):
    rows, cols = parts[0].shape
    return pl.pallas_call(
        place_kernel,
        grid_spec=pltpu.PrefetchScalarGridSpec(
            num_scalar_prefetch=2,
            grid=(1,),
            in_specs=[pl.BlockSpec((rows, cols), lambda t, s, w: (0, 0))] * 4,
            out_specs=pl.BlockSpec((owners, rows, block), lambda t, s, w: (0, 0, 0)),
        ),
        out_shape=jax.ShapeDtypeStruct((owners, rows, block), parts[0].dtype),
        compiler_params=pltpu.CompilerParams(vmem_limit_bytes=16 * MIB),
        cost_estimate=pl.CostEstimate(flops=rows * cols * 4, bytes_accessed=12 * rows * cols, transcendentals=0),
        name="place",
    )(idx, table, *parts)


def update_kernel(idx, *refs):
    low, high = refs[:8], refs[8:16]
    left, right, lroot, rroot, left_out, right_out, out, whole = refs[16:]
    j = pl.program_id(0)
    r = idx[0]
    y, core = r // 2, lax.rem(r, 2)

    def assemble(pieces):
        for c in range(2):
            for k, d in enumerate((0, 3, 1, 2)):
                row = 2 * lax.rem(y + d, 4) + (core if c == 0 else 1 - core)
                for q in range(4):
                    start = pl.multiple_of(q * 128 + row * 16, 16)
                    whole[pl.ds(start, 16), :] = pieces[4 * c + k][q]

    @pl.when(j < 4)
    def _():
        assemble(low)

    @pl.when(j >= 4)
    def _():
        assemble(high)

    scale = (1.0 - decay_rate) / whole.shape[0]
    share = left.shape[1]
    mine = whole[pl.ds(pl.multiple_of(r * share, share), share), :]
    stat_left = lax.dot_general(mine, whole[...], (((1,), (1,)), ((), ())), preferred_element_type=jnp.float32)
    left_out[0] = decay_rate * left[0] + scale * stat_left
    cols = whole[:, pl.ds(pl.multiple_of(y * 2 * share, 2 * share), 2 * share)]
    stat_right = lax.dot_general(cols, whole[...], (((0,), (0,)), ((), ())), preferred_element_type=jnp.float32)
    stat_right = jnp.where(core == 0, stat_right[:share], stat_right[share:])
    right_out[0] = decay_rate * right[0] + scale * stat_right
    half = jnp.dot(lroot[0], whole[...], preferred_element_type=jnp.float32).astype(jnp.bfloat16)
    out[0] = jnp.dot(half, rroot[0], preferred_element_type=jnp.float32).astype(out.dtype)


def update(idx, low, high, left, right, lroot, rroot):
    blocks, share, size = left.shape
    piece_low = pl.BlockSpec((4, 16, size), lambda j, s: (jnp.minimum(j, 3), 0, 0))
    piece_high = pl.BlockSpec((4, 16, size), lambda j, s: (jnp.maximum(j - 4, 0), 0, 0))
    thin = pl.BlockSpec((1, share, size), lambda j, s: (j, 0, 0))
    full = pl.BlockSpec((1, size, size), lambda j, s: (j, 0, 0))
    return pl.pallas_call(
        update_kernel,
        grid_spec=pltpu.PrefetchScalarGridSpec(
            num_scalar_prefetch=1,
            grid=(blocks,),
            in_specs=[piece_low] * 8 + [piece_high] * 8 + [thin, thin, thin, full],
            out_specs=[thin, thin, thin],
            scratch_shapes=[pltpu.VMEM((size, size), jnp.bfloat16)],
        ),
        out_shape=[
            jax.ShapeDtypeStruct(left.shape, left.dtype),
            jax.ShapeDtypeStruct(right.shape, right.dtype),
            jax.ShapeDtypeStruct(lroot.shape, lroot.dtype),
        ],
        compiler_params=pltpu.CompilerParams(vmem_limit_bytes=32 * MIB),
        cost_estimate=pl.CostEstimate(flops=blocks * 8 * share * size * size, bytes_accessed=14 * MIB, transcendentals=0),
        name="update",
    )(idx, *low, *high, left, right, lroot, rroot)


def shards(gradients, left_factor, right_factor, left_root, right_root, owner_table):
    owners = lax.axis_size("fsdp")
    block_size = left_factor.shape[-1]
    _, row_count, col_count = gradients.shape
    idx = jnp.stack([lax.axis_index("replica"), lax.axis_index("fsdp")]).astype(jnp.int32)

    swapped = permute(gradients, core_swap)
    grouped = (8, row_count // 8, col_count)
    kept, to_next, to_far, to_prev = pair_sum(idx, gradients.reshape(grouped), swapped.reshape(grouped))
    parts = [kept, permute(to_next, y_shift(1)), permute(to_far, y_shift(2)), permute(to_prev, y_shift(-1))]
    outgoing = place(idx, owner_table, parts, owners, block_size)
    received = lax.all_to_all(outgoing, "fsdp", split_axis=0, concat_axis=0, tiled=True)

    low, high = received[: owners // 2], received[owners // 2 :]
    low_prev = permute(low, y_shift(1))
    high_next = permute(high, y_shift(-1))
    high_prev = permute(high, y_shift(1))
    low_next = permute(low, y_shift(-1))
    low_far = permute(low_prev, y_shift(1))
    high_far = permute(high_next, y_shift(-1))
    low_pieces = [low, low_prev, low_next, low_far]
    high_pieces = [high, high_prev, high_next, high_far]
    low_pieces += [permute(p, core_swap) for p in low_pieces]
    high_pieces += [permute(p, core_swap) for p in high_pieces]

    left_new, right_new, result = update(
        idx, low_pieces, high_pieces, left_factor[0, 0], right_factor[0, 0], left_root[0, 0], right_root[0, 0]
    )
    return (left_new[None, None], right_new[None, None], result[None, None])


def solution(mesh):
    placed = (
        P("replica", "fsdp", None),
        P("fsdp", None, None, "replica", None),
        P("fsdp", None, None, "replica", None),
        P("fsdp", None, None, "replica", None),
        P("fsdp", None, None, None, None),
        P(),
    )
    return jax.shard_map(
        shards,
        mesh=mesh,
        in_specs=placed,
        out_specs=(
            P("fsdp", None, None, "replica", None),
            P("fsdp", None, None, "replica", None),
            P("fsdp", None, None, "replica", None),
        ),
        check_vma=False,
    )
```

time: 225 us -> 90.1 us (0.40)
  the two profiles are of different devices: /device:TPU:123 before, /device:TPU:1 now
where the time goes in v1:
time: 90.1 us; the launch traced here: 89.9 us
  waiting for transfers between devices  29.5 us (33%)
  starting transfers between devices  24.5 us (27%)
  blocking collectives  23.8 us (26%)
  Pallas kernels  9.71 us (11%)
  local copies, waits for them, and re-layouts  1.65 us (2%)
    ppermute x18, waiting for transfers between devices, permute(): return lax.ppermute(x, 'replica', pairs)  29.5 us
    ppermute x18, starting transfers between devices, permute(): return lax.ppermute(x, 'replica', pairs)  24.5 us
    all_to_all x1, blocking collectives, shards(): lax.all_to_all(outgoing, 'fsdp', split_axis=0, concat_axis=0, tiled=True)  23.8 us
    pallas_call x1, Pallas kernels, update(): pl.pallas_call(update_kernel, grid_spec=pltpu.PrefetchScalarGridSpec(num_...  7.09 us
    pallas_call x1, Pallas kernels, pair_sum(): pl.pallas_call(pair_sum_kernel, grid_spec=pltpu.PrefetchScalarGridSpec(nu...  1.86 us
  transfers between devices with their start and end apart: 18, of which 10 were waited for; matrix products, arithmetic and copies ran while one was open for 0% of the time, Pallas kernels for 0%

profile of v1, /device:TPU:1, one launch (start us, length us, event | category | flops | bytes accessed | tf_op | source)
XLA Modules:
  0.0 89.9 jit_solution(5257360514415580679)
XLA Ops:
  0.6 3.3 %collective-permute-start = (bf16[1,128,8192]{2,1,0:T(8,128)(2,1)}, bf16[1,128,8192]{2,1,0:T(8,128)(2,1)S(1)}, u32[]{:S(2)}, u32[]{:S(2)}) collective-permute-start(bf16[1,128,8192]{2,1,0:T(8,128)(2,1)} %param.6), channel_id=1, source_target_pairs={{0,32},{32,0},{64,96},{96,64},{128,160},{160,128},{192,224},{224,1... | collective-permute-start | bytes 6291464 | tf_op jit(solution)/shard_map/ppermute | solution.py:22
  4.0 3.9 %collective-permute-done = bf16[1,128,8192]{2,1,0:T(8,128)(2,1)S(1)} collective-permute-done((bf16[1,128,8192]{2,1,0:T(8,128)(2,1)}, bf16[1,128,8192]{2,1,0:T(8,128)(2,1)S(1)}, u32[]{:S(2)}, u32[]{:S(2)}) %collective-permute-start) | collective-permute-done | bytes 2097184 | tf_op jit(solution)/shard_map/ppermute | solution.py:22
  8.0 1.6 %copy-done = bf16[1,128,8192]{2,1,0:T(8,128)(2,1)S(1)} copy-done((bf16[1,128,8192]{2,1,0:T(8,128)(2,1)S(1)}, bf16[1,128,8192]{2,1,0:T(8,128)(2,1)}, u32[]{:S(2)}) %copy-start) | copy-done | bytes 2097176
  9.6 1.9 %pair_sum.1 = (bf16[16,8192]{1,0:T(8,128)(2,1)S(1)}, bf16[16,8192]{1,0:T(8,128)(2,1)S(1)}, bf16[16,8192]{1,0:T(8,128)(2,1)S(1)}, bf16[16,8192]{1,0:T(8,128)(2,1)S(1)}) custom-call(s32[2]{0:T(128)S(1)} %pad_add_fusion.idx, bf16[8,16,8192]{2,1,0:T(8,128)(2,1)S(1)} %bitcast.11, bf16[8,16,8192]{2,1,0:T(8,128)(2,1)S(1)} %bitcast.12, ...), custom_call_target="tpu_custom_call" | custom-call | flops 524288 | bytes 3145728 | tf_op jit(solution)/shard_map/pair_sum/pallas_call | solution.py:39
  11.5 2.2 %collective-permute-start.2 = (bf16[16,8192]{1,0:T(8,128)(2,1)S(1)}, bf16[16,8192]{1,0:T(8,128)(2,1)S(1)}, u32[]{:S(2)}, u32[]{:S(2)}) collective-permute-start(bf16[16,8192]{1,0:T(8,128)(2,1)S(1)} %get-tuple-element.12), channel_id=1, source_target_pairs={{0,128},{32,160},{64,192},{96,224},{128,0},{160,32},{192,64},{224,... | collective-permute-start | bytes 786440 | tf_op jit(solution)/shard_map/ppermute | solution.py:22
  13.7 1.1 %collective-permute-start.3 = (bf16[16,8192]{1,0:T(8,128)(2,1)S(1)}, bf16[16,8192]{1,0:T(8,128)(2,1)S(1)}, u32[]{:S(2)}, u32[]{:S(2)}) collective-permute-start(bf16[16,8192]{1,0:T(8,128)(2,1)S(1)} %get-tuple-element.13), channel_id=1, source_target_pairs={{0,192},{32,224},{64,0},{96,32},{128,64},{160,96},{192,128},{224,1... | collective-permute-start | bytes 786440 | tf_op jit(solution)/shard_map/ppermute | solution.py:22
  14.8 6.0 %collective-permute-done.1.b = bf16[16,8192]{1,0:T(8,128)(2,1)S(1)} collective-permute-done((bf16[16,8192]{1,0:T(8,128)(2,1)S(1)}, bf16[16,8192]{1,0:T(8,128)(2,1)S(1)}, u32[]{:S(2)}, u32[]{:S(2)}) %collective-permute-start.1) | collective-permute-done | bytes 262176 | tf_op jit(solution)/shard_map/ppermute | solution.py:22
  20.8 4.7 %collective-permute-done.2.c = bf16[16,8192]{1,0:T(8,128)(2,1)S(1)} collective-permute-done((bf16[16,8192]{1,0:T(8,128)(2,1)S(1)}, bf16[16,8192]{1,0:T(8,128)(2,1)S(1)}, u32[]{:S(2)}, u32[]{:S(2)}) %collective-permute-start.2) | collective-permute-done | bytes 262176 | tf_op jit(solution)/shard_map/ppermute | solution.py:22
  26.9 23.8 %all_to_all.5 = bf16[32,16,512]{2,1,0:T(8,128)(2,1)S(1)} all-to-all(bf16[32,16,512]{2,1,0:T(8,128)(2,1)S(1)} %place.1), channel_id=1, replica_groups=mesh['replica'=8,'fsdp'=32] {'fsdp'}, dimensions={0} | all-to-all | bytes 1048576 | tf_op jit(solution)/shard_map/all_to_all | solution.py:159
  50.8 4.6 %collective-permute-start.14 = (bf16[16,16,512]{2,1,0:T(8,128)(2,1)S(1)}, bf16[16,16,512]{2,1,0:T(8,128)(2,1)S(1)}, u32[]{:S(2)}, u32[]{:S(2)}) collective-permute-start(bf16[16,16,512]{2,1,0:T(8,128)(2,1)S(1)} %get-tuple-element.17.refs_8_), channel_id=1, source_target_pairs={{0,32},{32,0},{64,96},{96,64},{128,160},{160,128},{192,224},{224,1... | collective-permute-start | bytes 786440 | tf_op jit(solution)/shard_map/ppermute | solution.py:22
  55.4 1.9 %collective-permute-start.12 = (bf16[16,16,512]{2,1,0:T(8,128)(2,1)S(1)}, bf16[16,16,512]{2,1,0:T(8,128)(2,1)S(1)}, u32[]{:S(2)}, u32[]{:S(2)}) collective-permute-start(bf16[16,16,512]{2,1,0:T(8,128)(2,1)S(1)} %get-tuple-element.17.refs_8_), channel_id=1, source_target_pairs={{0,192},{32,224},{64,0},{96,32},{128,64},{160,96},{192,128},{224,1... | collective-permute-start | bytes 786440 | tf_op jit(solution)/shard_map/ppermute | solution.py:22
  57.8 0.9 %collective-permute-start.7 = (bf16[16,16,512]{2,1,0:T(8,128)(2,1)S(1)}, bf16[16,16,512]{2,1,0:T(8,128)(2,1)S(1)}, u32[]{:S(2)}, u32[]{:S(2)}) collective-permute-start(bf16[16,16,512]{2,1,0:T(8,128)(2,1)S(1)} %get-tuple-element.18.refs_0_), channel_id=1, source_target_pairs={{0,32},{32,0},{64,96},{96,64},{128,160},{160,128},{192,224},{224,1... | collective-permute-start | bytes 786440 | tf_op jit(solution)/shard_map/ppermute | solution.py:22
  58.7 1.9 %collective-permute-start.5 = (bf16[16,16,512]{2,1,0:T(8,128)(2,1)S(1)}, bf16[16,16,512]{2,1,0:T(8,128)(2,1)S(1)}, u32[]{:S(2)}, u32[]{:S(2)}) collective-permute-start(bf16[16,16,512]{2,1,0:T(8,128)(2,1)S(1)} %get-tuple-element.18.refs_0_), channel_id=1, source_target_pairs={{0,192},{32,224},{64,0},{96,32},{128,64},{160,96},{192,128},{224,1... | collective-permute-start | bytes 786440 | tf_op jit(solution)/shard_map/ppermute | solution.py:22
  60.7 2.6 %collective-permute-done.12.refs_10_ = bf16[16,16,512]{2,1,0:T(8,128)(2,1)S(1)} collective-permute-done((bf16[16,16,512]{2,1,0:T(8,128)(2,1)S(1)}, bf16[16,16,512]{2,1,0:T(8,128)(2,1)S(1)}, u32[]{:S(2)}, u32[]{:S(2)}) %collective-permute-start.12) | collective-permute-done | bytes 262176 | tf_op jit(solution)/shard_map/ppermute | solution.py:22
  63.3 1.3 %collective-permute-start.16 = (bf16[16,16,512]{2,1,0:T(8,128)(2,1)S(1)}, bf16[16,16,512]{2,1,0:T(8,128)(2,1)S(1)}, u32[]{:S(2)}, u32[]{:S(2)}) collective-permute-start(bf16[16,16,512]{2,1,0:T(8,128)(2,1)S(1)} %collective-permute-done.12.refs_10_), channel_id=1, source_target_pairs={{0,32},{32,0},{64,96},{96,64},{128,160},{160,128},{192,224},{224,1... | collective-permute-start | bytes 786440 | tf_op jit(solution)/shard_map/ppermute | solution.py:22
  64.6 1.5 %collective-permute-done.11.refs_9_ = bf16[16,16,512]{2,1,0:T(8,128)(2,1)S(1)} collective-permute-done((bf16[16,16,512]{2,1,0:T(8,128)(2,1)S(1)}, bf16[16,16,512]{2,1,0:T(8,128)(2,1)S(1)}, u32[]{:S(2)}, u32[]{:S(2)}) %collective-permute-start.11) | collective-permute-done | bytes 262176 | tf_op jit(solution)/shard_map/ppermute | solution.py:22
  66.1 1.7 %collective-permute-start.13 = (bf16[16,16,512]{2,1,0:T(8,128)(2,1)S(1)}, bf16[16,16,512]{2,1,0:T(8,128)(2,1)S(1)}, u32[]{:S(2)}, u32[]{:S(2)}) collective-permute-start(bf16[16,16,512]{2,1,0:T(8,128)(2,1)S(1)} %collective-permute-done.12.refs_10_), channel_id=1, source_target_pairs={{0,192},{32,224},{64,0},{96,32},{128,64},{160,96},{192,128},{224,1... | collective-permute-start | bytes 786440 | tf_op jit(solution)/shard_map/ppermute | solution.py:22
  67.7 4.0 %collective-permute-done.4.refs_1_ = bf16[16,16,512]{2,1,0:T(8,128)(2,1)S(1)} collective-permute-done((bf16[16,16,512]{2,1,0:T(8,128)(2,1)S(1)}, bf16[16,16,512]{2,1,0:T(8,128)(2,1)S(1)}, u32[]{:S(2)}, u32[]{:S(2)}) %collective-permute-start.4) | collective-permute-done | bytes 262176 | tf_op jit(solution)/shard_map/ppermute | solution.py:22
  71.7 1.2 %collective-permute-start.8 = (bf16[16,16,512]{2,1,0:T(8,128)(2,1)S(1)}, bf16[16,16,512]{2,1,0:T(8,128)(2,1)S(1)}, u32[]{:S(2)}, u32[]{:S(2)}) collective-permute-start(bf16[16,16,512]{2,1,0:T(8,128)(2,1)S(1)} %collective-permute-done.4.refs_1_), channel_id=1, source_target_pairs={{0,32},{32,0},{64,96},{96,64},{128,160},{160,128},{192,224},{224,1... | collective-permute-start | bytes 786440 | tf_op jit(solution)/shard_map/ppermute | solution.py:22
  74.2 1.2 %collective-permute-start.17 = (bf16[16,16,512]{2,1,0:T(8,128)(2,1)S(1)}, bf16[16,16,512]{2,1,0:T(8,128)(2,1)S(1)}, u32[]{:S(2)}, u32[]{:S(2)}) collective-permute-start(bf16[16,16,512]{2,1,0:T(8,128)(2,1)S(1)} %collective-permute-done.13.refs_11_), channel_id=1, source_target_pairs={{0,32},{32,0},{64,96},{96,64},{128,160},{160,128},{192,224},{224,1... | collective-permute-start | bytes 786440 | tf_op jit(solution)/shard_map/ppermute | solution.py:22
  75.4 4.1 %collective-permute-done.6.refs_3_ = bf16[16,16,512]{2,1,0:T(8,128)(2,1)S(1)} collective-permute-done((bf16[16,16,512]{2,1,0:T(8,128)(2,1)S(1)}, bf16[16,16,512]{2,1,0:T(8,128)(2,1)S(1)}, u32[]{:S(2)}, u32[]{:S(2)}) %collective-permute-start.6) | collective-permute-done | bytes 262176 | tf_op jit(solution)/shard_map/ppermute | solution.py:22
  79.5 2.1 %collective-permute-start.10 = (bf16[16,16,512]{2,1,0:T(8,128)(2,1)S(1)}, bf16[16,16,512]{2,1,0:T(8,128)(2,1)S(1)}, u32[]{:S(2)}, u32[]{:S(2)}) collective-permute-start(bf16[16,16,512]{2,1,0:T(8,128)(2,1)S(1)} %collective-permute-done.6.refs_3_), channel_id=1, source_target_pairs={{0,32},{32,0},{64,96},{96,64},{128,160},{160,128},{192,224},{224,1... | collective-permute-start | bytes 786440 | tf_op jit(solution)/shard_map/ppermute | solution.py:22
  81.7 1.1 %collective-permute-done.10.refs_7_ = bf16[16,16,512]{2,1,0:T(8,128)(2,1)S(1)} collective-permute-done((bf16[16,16,512]{2,1,0:T(8,128)(2,1)S(1)}, bf16[16,16,512]{2,1,0:T(8,128)(2,1)S(1)}, u32[]{:S(2)}, u32[]{:S(2)}) %collective-permute-start.10) | collective-permute-done | bytes 262176 | tf_op jit(solution)/shard_map/ppermute | solution.py:22
  82.8 7.1 %update.1 = (f32[8,64,512]{2,1,0:T(8,128)}, f32[8,64,512]{2,1,0:T(8,128)}, bf16[8,64,512]{2,1,0:T(8,128)(2,1)}) custom-call(s32[2]{0:T(128)S(1)} %pad_add_fusion.idx, bf16[16,16,512]{2,1,0:T(8,128)(2,1)S(1)} %get-tuple-element.18.refs_0_, bf16[16,16,512]{2,1,0:T(8,128)(2,1)S(1)} %collective-permute-done.4.refs_1_, ...), custom_call_target="tpu_custom_call" | custom-call | flops 1073741824 | bytes 14680064 | tf_op jit(solution)/shard_map/update/pallas_call | solution.py:128
  (30 shorter events, 3.6 us)
Async XLA Ops:
  0.6 7.3 %collective-permute-start = (bf16[1,128,8192]{2,1,0:T(8,128)(2,1)}, bf16[1,128,8192]{2,1,0:T(8,128)(2,1)S(1)}, u32[]{:S(2)}, u32[]{:S(2)}) collective-permute-start(bf16[1,128,8192]{2,1,0:T(8,128)(2,1)} %param.6), channel_id=1, source_target_pairs={{0,32},{32,0},{64,96},{96,64},{128,160},{160,128},{192,224},{224,1... | collective-permute-start | bytes 6291464 | tf_op jit(solution)/shard_map/ppermute | solution.py:22
  8.0 1.6 %copy-start = (bf16[1,128,8192]{2,1,0:T(8,128)(2,1)S(1)}, bf16[1,128,8192]{2,1,0:T(8,128)(2,1)}, u32[]{:S(2)}) copy-start(bf16[1,128,8192]{2,1,0:T(8,128)(2,1)} %param.6) | copy-start | bytes 6291460
  9.5 16.6 %copy-start.5 = (s32[8,16]{1,0:T(8,128)S(1)}, s32[8,16]{1,0:T(8,128)}, u32[]{:S(2)}) copy-start(s32[8,16]{1,0:T(8,128)} %table.1) | copy-start | bytes 1540
  9.5 73.2 %copy-start.1 = (bf16[1,1,8,512,512]{4,3,2,1,0:T(8,128)(2,1)S(1)}, bf16[1,1,8,512,512]{4,3,2,1,0:T(8,128)(2,1)}, u32[]{:S(2)}) copy-start(bf16[1,1,8,512,512]{4,3,2,1,0:T(8,128)(2,1)} %param.10) | copy-start | bytes 12582916
  11.4 71.4 %copy-start.2 = (f32[1,1,8,64,512]{4,3,2,1,0:T(8,128)S(1)}, f32[1,1,8,64,512]{4,3,2,1,0:T(8,128)}, u32[]{:S(2)}) copy-start(f32[1,1,8,64,512]{4,3,2,1,0:T(8,128)} %param.7) | copy-start | bytes 3145732
  11.4 71.4 %copy-start.3 = (f32[1,1,8,64,512]{4,3,2,1,0:T(8,128)S(1)}, f32[1,1,8,64,512]{4,3,2,1,0:T(8,128)}, u32[]{:S(2)}) copy-start(f32[1,1,8,64,512]{4,3,2,1,0:T(8,128)} %param.8) | copy-start | bytes 3145732
  11.4 71.4 %copy-start.4 = (bf16[1,1,8,64,512]{4,3,2,1,0:T(8,128)(2,1)S(1)}, bf16[1,1,8,64,512]{4,3,2,1,0:T(8,128)(2,1)}, u32[]{:S(2)}) copy-start(bf16[1,1,8,64,512]{4,3,2,1,0:T(8,128)(2,1)} %param.9) | copy-start | bytes 1572868
  11.5 9.3 %collective-permute-start.1 = (bf16[16,8192]{1,0:T(8,128)(2,1)S(1)}, bf16[16,8192]{1,0:T(8,128)(2,1)S(1)}, u32[]{:S(2)}, u32[]{:S(2)}) collective-permute-start(bf16[16,8192]{1,0:T(8,128)(2,1)S(1)} %get-tuple-element.11), channel_id=1, source_target_pairs={{0,64},{32,96},{64,128},{96,160},{128,192},{160,224},{192,0},{224,... | collective-permute-start | bytes 786440 | tf_op jit(solution)/shard_map/ppermute | solution.py:22
  11.5 13.9 %collective-permute-start.2 = (bf16[16,8192]{1,0:T(8,128)(2,1)S(1)}, bf16[16,8192]{1,0:T(8,128)(2,1)S(1)}, u32[]{:S(2)}, u32[]{:S(2)}) collective-permute-start(bf16[16,8192]{1,0:T(8,128)(2,1)S(1)} %get-tuple-element.12), channel_id=1, source_target_pairs={{0,128},{32,160},{64,192},{96,224},{128,0},{160,32},{192,64},{224,... | collective-permute-start | bytes 786440 | tf_op jit(solution)/shard_map/ppermute | solution.py:22
  13.7 12.5 %collective-permute-start.3 = (bf16[16,8192]{1,0:T(8,128)(2,1)S(1)}, bf16[16,8192]{1,0:T(8,128)(2,1)S(1)}, u32[]{:S(2)}, u32[]{:S(2)}) collective-permute-start(bf16[16,8192]{1,0:T(8,128)(2,1)S(1)} %get-tuple-element.13), channel_id=1, source_target_pairs={{0,192},{32,224},{64,0},{96,32},{128,64},{160,96},{192,128},{224,1... | collective-permute-start | bytes 786440 | tf_op jit(solution)/shard_map/ppermute | solution.py:22
  50.8 8.0 %collective-permute-start.14 = (bf16[16,16,512]{2,1,0:T(8,128)(2,1)S(1)}, bf16[16,16,512]{2,1,0:T(8,128)(2,1)S(1)}, u32[]{:S(2)}, u32[]{:S(2)}) collective-permute-start(bf16[16,16,512]{2,1,0:T(8,128)(2,1)S(1)} %get-tuple-element.17.refs_8_), channel_id=1, source_target_pairs={{0,32},{32,0},{64,96},{96,64},{128,160},{160,128},{192,224},{224,1... | collective-permute-start | bytes 786440 | tf_op jit(solution)/shard_map/ppermute | solution.py:22
  55.4 7.9 %collective-permute-start.12 = (bf16[16,16,512]{2,1,0:T(8,128)(2,1)S(1)}, bf16[16,16,512]{2,1,0:T(8,128)(2,1)S(1)}, u32[]{:S(2)}, u32[]{:S(2)}) collective-permute-start(bf16[16,16,512]{2,1,0:T(8,128)(2,1)S(1)} %get-tuple-element.17.refs_8_), channel_id=1, source_target_pairs={{0,192},{32,224},{64,0},{96,32},{128,64},{160,96},{192,128},{224,1... | collective-permute-start | bytes 786440 | tf_op jit(solution)/shard_map/ppermute | solution.py:22
  57.3 8.7 %collective-permute-start.11 = (bf16[16,16,512]{2,1,0:T(8,128)(2,1)S(1)}, bf16[16,16,512]{2,1,0:T(8,128)(2,1)S(1)}, u32[]{:S(2)}, u32[]{:S(2)}) collective-permute-start(bf16[16,16,512]{2,1,0:T(8,128)(2,1)S(1)} %get-tuple-element.17.refs_8_), channel_id=1, source_target_pairs={{0,64},{32,96},{64,128},{96,160},{128,192},{160,224},{192,0},{224,... | collective-permute-start | bytes 786440 | tf_op jit(solution)/shard_map/ppermute | solution.py:22
  57.3 14.4 %collective-permute-start.4 = (bf16[16,16,512]{2,1,0:T(8,128)(2,1)S(1)}, bf16[16,16,512]{2,1,0:T(8,128)(2,1)S(1)}, u32[]{:S(2)}, u32[]{:S(2)}) collective-permute-start(bf16[16,16,512]{2,1,0:T(8,128)(2,1)S(1)} %get-tuple-element.18.refs_0_), channel_id=1, source_target_pairs={{0,64},{32,96},{64,128},{96,160},{128,192},{160,224},{192,0},{224,... | collective-permute-start | bytes 786440 | tf_op jit(solution)/shard_map/ppermute | solution.py:22
  57.8 13.9 %collective-permute-start.7 = (bf16[16,16,512]{2,1,0:T(8,128)(2,1)S(1)}, bf16[16,16,512]{2,1,0:T(8,128)(2,1)S(1)}, u32[]{:S(2)}, u32[]{:S(2)}) collective-permute-start(bf16[16,16,512]{2,1,0:T(8,128)(2,1)S(1)} %get-tuple-element.18.refs_0_), channel_id=1, source_target_pairs={{0,32},{32,0},{64,96},{96,64},{128,160},{160,128},{192,224},{224,1... | collective-permute-start | bytes 786440 | tf_op jit(solution)/shard_map/ppermute | solution.py:22
  58.7 14.1 %collective-permute-start.5 = (bf16[16,16,512]{2,1,0:T(8,128)(2,1)S(1)}, bf16[16,16,512]{2,1,0:T(8,128)(2,1)S(1)}, u32[]{:S(2)}, u32[]{:S(2)}) collective-permute-start(bf16[16,16,512]{2,1,0:T(8,128)(2,1)S(1)} %get-tuple-element.18.refs_0_), channel_id=1, source_target_pairs={{0,192},{32,224},{64,0},{96,32},{128,64},{160,96},{192,128},{224,1... | collective-permute-start | bytes 786440 | tf_op jit(solution)/shard_map/ppermute | solution.py:22
  63.3 9.7 %collective-permute-start.16 = (bf16[16,16,512]{2,1,0:T(8,128)(2,1)S(1)}, bf16[16,16,512]{2,1,0:T(8,128)(2,1)S(1)}, u32[]{:S(2)}, u32[]{:S(2)}) collective-permute-start(bf16[16,16,512]{2,1,0:T(8,128)(2,1)S(1)} %collective-permute-done.12.refs_10_), channel_id=1, source_target_pairs={{0,32},{32,0},{64,96},{96,64},{128,160},{160,128},{192,224},{224,1... | collective-permute-start | bytes 786440 | tf_op jit(solution)/shard_map/ppermute | solution.py:22
  66.1 8.1 %collective-permute-start.13 = (bf16[16,16,512]{2,1,0:T(8,128)(2,1)S(1)}, bf16[16,16,512]{2,1,0:T(8,128)(2,1)S(1)}, u32[]{:S(2)}, u32[]{:S(2)}) collective-permute-start(bf16[16,16,512]{2,1,0:T(8,128)(2,1)S(1)} %collective-permute-done.12.refs_10_), channel_id=1, source_target_pairs={{0,192},{32,224},{64,0},{96,32},{128,64},{160,96},{192,128},{224,1... | collective-permute-start | bytes 786440 | tf_op jit(solution)/shard_map/ppermute | solution.py:22
  71.7 7.8 %collective-permute-start.6 = (bf16[16,16,512]{2,1,0:T(8,128)(2,1)S(1)}, bf16[16,16,512]{2,1,0:T(8,128)(2,1)S(1)}, u32[]{:S(2)}, u32[]{:S(2)}) collective-permute-start(bf16[16,16,512]{2,1,0:T(8,128)(2,1)S(1)} %collective-permute-done.4.refs_1_), channel_id=1, source_target_pairs={{0,64},{32,96},{64,128},{96,160},{128,192},{160,224},{192,0},{224,... | collective-permute-start | bytes 786440 | tf_op jit(solution)/shard_map/ppermute | solution.py:22
  71.7 9.9 %collective-permute-start.8 = (bf16[16,16,512]{2,1,0:T(8,128)(2,1)S(1)}, bf16[16,16,512]{2,1,0:T(8,128)(2,1)S(1)}, u32[]{:S(2)}, u32[]{:S(2)}) collective-permute-start(bf16[16,16,512]{2,1,0:T(8,128)(2,1)S(1)} %collective-permute-done.4.refs_1_), channel_id=1, source_target_pairs={{0,32},{32,0},{64,96},{96,64},{128,160},{160,128},{192,224},{224,1... | collective-permute-start | bytes 786440 | tf_op jit(solution)/shard_map/ppermute | solution.py:22
  72.9 8.7 %collective-permute-start.15 = (bf16[16,16,512]{2,1,0:T(8,128)(2,1)S(1)}, bf16[16,16,512]{2,1,0:T(8,128)(2,1)S(1)}, u32[]{:S(2)}, u32[]{:S(2)}) collective-permute-start(bf16[16,16,512]{2,1,0:T(8,128)(2,1)S(1)} %collective-permute-done.11.refs_9_), channel_id=1, source_target_pairs={{0,32},{32,0},{64,96},{96,64},{128,160},{160,128},{192,224},{224,1... | collective-permute-start | bytes 786440 | tf_op jit(solution)/shard_map/ppermute | solution.py:22
  73.0 8.6 %collective-permute-start.9 = (bf16[16,16,512]{2,1,0:T(8,128)(2,1)S(1)}, bf16[16,16,512]{2,1,0:T(8,128)(2,1)S(1)}, u32[]{:S(2)}, u32[]{:S(2)}) collective-permute-start(bf16[16,16,512]{2,1,0:T(8,128)(2,1)S(1)} %collective-permute-done.5.refs_2_), channel_id=1, source_target_pairs={{0,32},{32,0},{64,96},{96,64},{128,160},{160,128},{192,224},{224,1... | collective-permute-start | bytes 786440 | tf_op jit(solution)/shard_map/ppermute | solution.py:22
  74.2 7.4 %collective-permute-start.17 = (bf16[16,16,512]{2,1,0:T(8,128)(2,1)S(1)}, bf16[16,16,512]{2,1,0:T(8,128)(2,1)S(1)}, u32[]{:S(2)}, u32[]{:S(2)}) collective-permute-start(bf16[16,16,512]{2,1,0:T(8,128)(2,1)S(1)} %collective-permute-done.13.refs_11_), channel_id=1, source_target_pairs={{0,32},{32,0},{64,96},{96,64},{128,160},{160,128},{192,224},{224,1... | collective-permute-start | bytes 786440 | tf_op jit(solution)/shard_map/ppermute | solution.py:22
  79.5 3.3 %collective-permute-start.10 = (bf16[16,16,512]{2,1,0:T(8,128)(2,1)S(1)}, bf16[16,16,512]{2,1,0:T(8,128)(2,1)S(1)}, u32[]{:S(2)}, u32[]{:S(2)}) collective-permute-start(bf16[16,16,512]{2,1,0:T(8,128)(2,1)S(1)} %collective-permute-done.6.refs_3_), channel_id=1, source_target_pairs={{0,32},{32,0},{64,96},{96,64},{128,160},{160,128},{192,224},{224,1... | collective-permute-start | bytes 786440 | tf_op jit(solution)/shard_map/ppermute | solution.py:22

commit v2 on v0

v2 whole, which is shorter than its diff:
```python
import jax
import jax.numpy as jnp
from jax import lax
from jax.experimental import pallas as pl
from jax.experimental.pallas import tpu as pltpu
from jax.sharding import PartitionSpec as P

decay_rate = 0.9
MIB = 1 << 20
SPLIT = 4
VMEM = pl.BlockSpec(memory_space=pltpu.VMEM)
SMEM = pl.BlockSpec(memory_space=pltpu.SMEM)
HBM = pl.BlockSpec(memory_space=pltpu.HBM)

core_swap = [(r, r ^ 1) for r in range(8)]
split_ring = [(r, (r + 2 - 4 * (r % 2)) % 8) for r in range(8)]


def y_shift(d):
    return [(r, (r + 2 * d) % 8) for r in range(8)]


def permute(x, pairs):
    return lax.ppermute(x, "replica", pairs)


def group_of(r, k):
    return 2 * lax.rem(r // 2 + k, 4) + lax.rem(r, 2)


def own_rows_kernel(grads, out, sems):
    copies = [pltpu.make_async_copy(grads.at[group_of(lax.axis_index("replica"), k)], out.at[k], sems.at[k]) for k in range(4)]
    for c in copies:
        c.start()
    for c in copies:
        c.wait()


def own_rows(grads):
    _, rows, cols = grads.shape
    return pl.pallas_call(
        own_rows_kernel,
        in_specs=[HBM],
        out_specs=VMEM,
        out_shape=jax.ShapeDtypeStruct((4, rows, cols), grads.dtype),
        scratch_shapes=[pltpu.SemaphoreType.DMA((4,))],
        compiler_params=pltpu.CompilerParams(vmem_limit_bytes=8 * MIB),
        cost_estimate=pl.CostEstimate(flops=0, bytes_accessed=4 * MIB, transcendentals=0),
        name="own_rows",
    )(grads)


def pair_sum_kernel(own, recv, *outs):
    for k in range(4):
        total = own[k].astype(jnp.float32) + recv[group_of(lax.axis_index("replica"), k)].astype(jnp.float32)
        outs[k][...] = total.astype(own.dtype)


def pair_sum(own, recv, block):
    _, rows, cols = own.shape
    return pl.pallas_call(
        pair_sum_kernel,
        in_specs=[VMEM, VMEM],
        out_specs=[VMEM] * 4,
        out_shape=[jax.ShapeDtypeStruct((rows, cols), own.dtype)] * 4,
        compiler_params=pltpu.CompilerParams(vmem_limit_bytes=8 * MIB),
        cost_estimate=pl.CostEstimate(flops=4 * rows * cols, bytes_accessed=4 * MIB, transcendentals=0),
        name="pair_sum",
    )(own, recv)


def place_kernel(table, *refs):
    halves = len(refs) // 5
    my_row = lax.axis_index("fsdp") // 4
    for h in range(halves):
        a, b, c, d = refs[4 * h : 4 * h + 4]
        out = refs[4 * halves + h]
        width = out.shape[-1]
        out[...] = jnp.zeros_like(out)
        for col in range(a.shape[-1] // width):
            cut = slice(col * width, (col + 1) * width)
            total = (
                a[:, cut].astype(jnp.float32)
                + b[:, cut].astype(jnp.float32)
                + c[:, cut].astype(jnp.float32)
                + d[:, cut].astype(jnp.float32)
            )
            out[table[my_row, col]] = total.astype(out.dtype)


def place(table, parts, owners, width):
    rows, cols = parts[0].shape
    halves = len(parts) // 4
    return pl.pallas_call(
        place_kernel,
        in_specs=[SMEM] + [VMEM] * len(parts),
        out_specs=[VMEM] * halves,
        out_shape=[jax.ShapeDtypeStruct((owners, rows, width), parts[0].dtype)] * halves,
        compiler_params=pltpu.CompilerParams(vmem_limit_bytes=8 * MIB),
        cost_estimate=pl.CostEstimate(flops=4 * rows * cols * halves, bytes_accessed=MIB * halves, transcendentals=0),
        name="place",
    )(table, *parts)


def update_kernel(first, *refs):
    pieces, (left, right, lroot, rroot) = refs[: len(places)], refs[len(places) : len(places) + 4]
    left_out, right_out, out, whole, left_new, right_new, result, sems = refs[-8:]
    r = lax.axis_index("replica")
    y, core = r // 2, lax.rem(r, 2)
    count, share, size = left_new.shape
    quarter = size // 4
    scale = (1.0 - decay_rate) / size
    sends = []
    for n in range(count):
        j = first + n
        block = whole.at[n]
        for piece, (ahead, dy, flip) in zip(pieces, places):
            row = 2 * lax.rem(y + dy + ahead * (2 * core - 1) + 4, 4) + (1 - core if flip else core)
            for q in range(4):
                start = pl.multiple_of(q * quarter + row * 16, 16)
                block[pl.ds(start, 16), :] = piece[4 * n + q]
        mine = block[pl.ds(pl.multiple_of(r * share, share), share), :]
        stat_left = lax.dot_general(mine, block[...], (((1,), (1,)), ((), ())), preferred_element_type=jnp.float32)
        left_new[n] = decay_rate * left[j] + scale * stat_left
        turned = block[:, pl.ds(pl.multiple_of(y * 2 * share, 2 * share), 2 * share)].T
        turned = jnp.where(core == 0, turned[:share], turned[share:])
        both = jnp.dot(jnp.concatenate([turned, lroot[j]], axis=0), block[...], preferred_element_type=jnp.float32)
        right_new[n] = decay_rate * right[j] + scale * both[:share]
        half = both[share:].astype(jnp.bfloat16)
        result[n] = jnp.dot(half, rroot[j], preferred_element_type=jnp.float32).astype(result.dtype)
        for m, (src, dst) in enumerate(((left_new, left_out), (right_new, right_out), (result, out))):
            sends.append(pltpu.make_async_copy(src.at[n], dst.at[j], sems.at[m, n]))
            sends[-1].start()
    for send in sends:
        send.wait()


def update(first, count, pieces, left, right, lroot, rroot, earlier):
    _, share, size = left.shape
    shapes = [jax.ShapeDtypeStruct(x.shape, x.dtype) for x in (left, right, lroot)]
    return pl.pallas_call(
        lambda *refs: update_kernel(first, *refs),
        in_specs=[VMEM] * (len(pieces) + 4) + [HBM] * len(earlier),
        out_specs=[HBM] * 3,
        out_shape=shapes,
        scratch_shapes=[pltpu.VMEM((count, size, size), lroot.dtype)]
        + [pltpu.VMEM((count, share, size), x.dtype) for x in shapes]
        + [pltpu.SemaphoreType.DMA((3, count))],
        input_output_aliases={len(pieces) + 4 + n: n for n in range(len(earlier))},
        compiler_params=pltpu.CompilerParams(vmem_limit_bytes=16 * MIB),
        cost_estimate=pl.CostEstimate(flops=count * 8 * share * size * size, bytes_accessed=2 * count * MIB, transcendentals=0),
        name="update",
    )(*pieces, left, right, lroot, rroot, *earlier)


def tie(*xs):
    return lax.optimization_barrier(xs)


def cross(x):
    return permute(x, core_swap)


def gather(own, split):
    parts = [own[: 4 * split], own[4 * split :]]
    groups = []
    for n, part in enumerate(parts):
        a, b = tie(part, cross(part))
        near, near_other = permute(a, split_ring), permute(b, split_ring)
        far = permute(near, split_ring)
        groups.append([part, b, near, near_other, cross(near), cross(near_other), far])
    return groups


places = ((0, 0, 0), (0, 0, 1), (1, 0, 0), (1, 0, 1), (-1, 0, 1), (-1, 0, 0), (0, 2, 0), (0, 2, 1))


def shards(gradients, left_factor, right_factor, left_root, right_root, owner_table):
    owners = lax.axis_size("fsdp")
    block = left_factor.shape[-1]
    _, row_count, col_count = gradients.shape

    swapped = permute(gradients, core_swap)
    grouped = (8, row_count // 8, col_count)
    own = own_rows(gradients.reshape(grouped))
    sums = pair_sum(own, swapped.reshape(grouped), block)
    kept, to_next, to_far, to_prev = sums
    parts = [kept, permute(to_far, y_shift(2)), permute(to_next, y_shift(1)), permute(to_prev, y_shift(-1))]
    (outgoing,) = place(owner_table, parts, owners, block)
    received = lax.all_to_all(outgoing, "fsdp", split_axis=0, concat_axis=0, tiled=True)
    factors = (left_factor[0, 0], right_factor[0, 0], left_root[0, 0], right_root[0, 0])
    blocks = owners // 4
    low, high = gather(received, SPLIT)
    low.append(cross(low[-1]))
    results = update(0, SPLIT, low, *factors, [])
    high.append(cross(high[-1]))
    left_new, right_new, result = update(SPLIT, blocks - SPLIT, high, *factors, results)
    return (left_new[None, None], right_new[None, None], result[None, None])


def solution(mesh):
    placed = (
        P("replica", "fsdp", None),
        P("fsdp", None, None, "replica", None),
        P("fsdp", None, None, "replica", None),
        P("fsdp", None, None, "replica", None),
        P("fsdp", None, None, None, None),
        P(),
    )
    return jax.shard_map(
        shards,
        mesh=mesh,
        in_specs=placed,
        out_specs=(
            P("fsdp", None, None, "replica", None),
            P("fsdp", None, None, "replica", None),
            P("fsdp", None, None, "replica", None),
        ),
        check_vma=False,
    )
```

time: 225 us -> 80.6 us (0.36)
  the two profiles are of different devices: /device:TPU:123 before, /device:TPU:1 now
where the time goes in v2:
time: 80.6 us; the launch traced here: 80.5 us
  starting transfers between devices  29.5 us (37%)
  blocking collectives  23.1 us (29%)
  waiting for transfers between devices  18.8 us (23%)
  Pallas kernels  6.49 us (8%)
  local copies, waits for them, and re-layouts  1.65 us (2%)
  between operations  0.92 us (1%)
    ppermute x18, starting transfers between devices, permute(): return lax.ppermute(x, 'replica', pairs)  29.5 us
    all_to_all x1, blocking collectives, shards(): lax.all_to_all(outgoing, 'fsdp', split_axis=0, concat_axis=0, tiled=True)  23.1 us
    ppermute x18, waiting for transfers between devices, permute(): return lax.ppermute(x, 'replica', pairs)  18.8 us
    pallas_call x2, Pallas kernels, update(): pl.pallas_call(lambda *refs: update_kernel(first, *refs), in_specs=[VMEM]...  5.36 us
    unnamed x12, local copies, waits for them, and re-layouts  1.62 us
  transfers between devices with their start and end apart: 18, of which 8 were waited for; matrix products, arithmetic and copies ran while one was open for 0% of the time, Pallas kernels for 3%

profile of v2, /device:TPU:1, one launch (start us, length us, event | category | flops | bytes accessed | tf_op | source)
XLA Modules:
  0.0 80.5 jit_solution(15985145137314489326)
XLA Ops:
  0.6 3.3 %collective-permute-start = (bf16[1,128,8192]{2,1,0:T(8,128)(2,1)}, bf16[1,128,8192]{2,1,0:T(8,128)(2,1)S(1)}, u32[]{:S(2)}, u32[]{:S(2)}) collective-permute-start(bf16[1,128,8192]{2,1,0:T(8,128)(2,1)} %param.6), channel_id=1, source_target_pairs={{0,32},{32,0},{64,96},{96,64},{128,160},{160,128},{192,224},{224,1... | collective-permute-start | bytes 6291464 | tf_op jit(solution)/shard_map/ppermute | solution.py:24
  4.0 1.6 %copy-done.4 = bf16[1,128,8192]{2,1,0:T(8,128)(2,1)S(1)} copy-done((bf16[1,128,8192]{2,1,0:T(8,128)(2,1)S(1)}, bf16[1,128,8192]{2,1,0:T(8,128)(2,1)}, u32[]{:S(2)}) %copy-start.4) | copy-done | bytes 2097176
  5.7 2.3 %collective-permute-done = bf16[1,128,8192]{2,1,0:T(8,128)(2,1)S(1)} collective-permute-done((bf16[1,128,8192]{2,1,0:T(8,128)(2,1)}, bf16[1,128,8192]{2,1,0:T(8,128)(2,1)S(1)}, u32[]{:S(2)}, u32[]{:S(2)}) %collective-permute-start) | collective-permute-done | bytes 2097184 | tf_op jit(solution)/shard_map/ppermute | solution.py:24
  8.3 1.3 %collective-permute-start.1 = (bf16[16,8192]{1,0:T(8,128)(2,1)S(1)}, bf16[16,8192]{1,0:T(8,128)(2,1)S(1)}, u32[]{:S(2)}, u32[]{:S(2)}) collective-permute-start(bf16[16,8192]{1,0:T(8,128)(2,1)S(1)} %get-tuple-element.18), channel_id=1, source_target_pairs={{0,128},{32,160},{64,192},{96,224},{128,0},{160,32},{192,64},{224,... | collective-permute-start | bytes 786440 | tf_op jit(solution)/shard_map/ppermute | solution.py:24
  9.9 2.3 %collective-permute-start.3 = (bf16[16,8192]{1,0:T(8,128)(2,1)S(1)}, bf16[16,8192]{1,0:T(8,128)(2,1)S(1)}, u32[]{:S(2)}, u32[]{:S(2)}) collective-permute-start(bf16[16,8192]{1,0:T(8,128)(2,1)S(1)} %get-tuple-element.20), channel_id=1, source_target_pairs={{0,192},{32,224},{64,0},{96,32},{128,64},{160,96},{192,128},{224,1... | collective-permute-start | bytes 786440 | tf_op jit(solution)/shard_map/ppermute | solution.py:24
  12.2 5.2 %collective-permute-done.1.refs_1_ = bf16[16,8192]{1,0:T(8,128)(2,1)S(1)} collective-permute-done((bf16[16,8192]{1,0:T(8,128)(2,1)S(1)}, bf16[16,8192]{1,0:T(8,128)(2,1)S(1)}, u32[]{:S(2)}, u32[]{:S(2)}) %collective-permute-start.1) | collective-permute-done | bytes 262176 | tf_op jit(solution)/shard_map/ppermute | solution.py:24
  17.4 6.3 %collective-permute-done.2.refs_2_ = bf16[16,8192]{1,0:T(8,128)(2,1)S(1)} collective-permute-done((bf16[16,8192]{1,0:T(8,128)(2,1)S(1)}, bf16[16,8192]{1,0:T(8,128)(2,1)S(1)}, u32[]{:S(2)}, u32[]{:S(2)}) %collective-permute-start.2) | collective-permute-done | bytes 262176 | tf_op jit(solution)/shard_map/ppermute | solution.py:24
  23.7 0.8 place.1
  24.5 23.1 %all_to_all.5 = bf16[32,16,512]{2,1,0:T(8,128)(2,1)S(1)} all-to-all(bf16[32,16,512]{2,1,0:T(8,128)(2,1)S(1)} %place.1), channel_id=1, replica_groups=mesh['replica'=8,'fsdp'=32] {'fsdp'}, dimensions={0} | all-to-all | bytes 1048576 | tf_op jit(solution)/shard_map/all_to_all | solution.py:190
  47.6 4.1 %collective-permute-start.11 = (bf16[16,16,512]{2,1,0:T(8,128)(2,1)S(1)}, bf16[16,16,512]{2,1,0:T(8,128)(2,1)S(1)}, u32[]{:S(2)}, u32[]{:S(2)}) collective-permute-start(bf16[16,16,512]{2,1,0:T(8,128)(2,1)S(1)} %get-tuple-element.24.refs_0_), channel_id=1, source_target_pairs={{0,32},{32,0},{64,96},{96,64},{128,160},{160,128},{192,224},{224,1... | collective-permute-start | bytes 786440 | tf_op jit(solution)/shard_map/ppermute | solution.py:24
  51.8 1.1 %collective-permute-done.11.refs_1_ = bf16[16,16,512]{2,1,0:T(8,128)(2,1)S(1)} collective-permute-done((bf16[16,16,512]{2,1,0:T(8,128)(2,1)S(1)}, bf16[16,16,512]{2,1,0:T(8,128)(2,1)S(1)}, u32[]{:S(2)}, u32[]{:S(2)}) %collective-permute-start.11) | collective-permute-done | bytes 262176 | tf_op jit(solution)/shard_map/ppermute | solution.py:24
  52.9 2.3 %collective-permute-start.12 = (bf16[16,16,512]{2,1,0:T(8,128)(2,1)S(1)}, bf16[16,16,512]{2,1,0:T(8,128)(2,1)S(1)}, u32[]{:S(2)}, u32[]{:S(2)}) collective-permute-start(bf16[16,16,512]{2,1,0:T(8,128)(2,1)S(1)} %get-tuple-element.24.refs_0_), channel_id=1, source_target_pairs={{0,64},{32,224},{64,128},{96,32},{128,192},{160,96},{192,0},{224,1... | collective-permute-start | bytes 786440 | tf_op jit(solution)/shard_map/ppermute | solution.py:24
  55.9 2.6 %collective-permute-done.12.refs_2_ = bf16[16,16,512]{2,1,0:T(8,128)(2,1)S(1)} collective-permute-done((bf16[16,16,512]{2,1,0:T(8,128)(2,1)S(1)}, bf16[16,16,512]{2,1,0:T(8,128)(2,1)S(1)}, u32[]{:S(2)}, u32[]{:S(2)}) %collective-permute-start.12) | collective-permute-done | bytes 262176 | tf_op jit(solution)/shard_map/ppermute | solution.py:24
  58.5 3.1 %collective-permute-start.16 = (bf16[16,16,512]{2,1,0:T(8,128)(2,1)S(1)}, bf16[16,16,512]{2,1,0:T(8,128)(2,1)S(1)}, u32[]{:S(2)}, u32[]{:S(2)}) collective-permute-start(bf16[16,16,512]{2,1,0:T(8,128)(2,1)S(1)} %collective-permute-done.12.refs_2_), channel_id=1, source_target_pairs={{0,64},{32,224},{64,128},{96,32},{128,192},{160,96},{192,0},{224,1... | collective-permute-start | bytes 786440 | tf_op jit(solution)/shard_map/ppermute | solution.py:24
  61.7 2.8 %collective-permute-start.9 = (bf16[16,16,512]{2,1,0:T(8,128)(2,1)S(1)}, bf16[16,16,512]{2,1,0:T(8,128)(2,1)S(1)}, u32[]{:S(2)}, u32[]{:S(2)}) collective-permute-start(bf16[16,16,512]{2,1,0:T(8,128)(2,1)S(1)} %collective-permute-done.5.refs_2_), channel_id=1, source_target_pairs={{0,64},{32,224},{64,128},{96,32},{128,192},{160,96},{192,0},{224,1... | collective-permute-start | bytes 786440 | tf_op jit(solution)/shard_map/ppermute | solution.py:24
  64.4 2.0 %collective-permute-start.15 = (bf16[16,16,512]{2,1,0:T(8,128)(2,1)S(1)}, bf16[16,16,512]{2,1,0:T(8,128)(2,1)S(1)}, u32[]{:S(2)}, u32[]{:S(2)}) collective-permute-start(bf16[16,16,512]{2,1,0:T(8,128)(2,1)S(1)} %collective-permute-done.13.refs_3_), channel_id=1, source_target_pairs={{0,32},{32,0},{64,96},{96,64},{128,160},{160,128},{192,224},{224,1... | collective-permute-start | bytes 786440 | tf_op jit(solution)/shard_map/ppermute | solution.py:24
  66.5 0.5 collective-permute-done.16.refs_6_
  66.9 2.4 %collective-permute-start.17 = (bf16[16,16,512]{2,1,0:T(8,128)(2,1)S(1)}, bf16[16,16,512]{2,1,0:T(8,128)(2,1)S(1)}, u32[]{:S(2)}, u32[]{:S(2)}) collective-permute-start(bf16[16,16,512]{2,1,0:T(8,128)(2,1)S(1)} %collective-permute-done.16.refs_6_), channel_id=1, source_target_pairs={{0,32},{32,0},{64,96},{96,64},{128,160},{160,128},{192,224},{224,1... | collective-permute-start | bytes 786440 | tf_op jit(solution)/shard_map/ppermute | solution.py:24
  69.3 0.5 collective-permute-done.6.refs_3_
  69.7 2.4 %collective-permute-start.7 = (bf16[16,16,512]{2,1,0:T(8,128)(2,1)S(1)}, bf16[16,16,512]{2,1,0:T(8,128)(2,1)S(1)}, u32[]{:S(2)}, u32[]{:S(2)}) collective-permute-start(bf16[16,16,512]{2,1,0:T(8,128)(2,1)S(1)} %collective-permute-done.5.refs_2_), channel_id=1, source_target_pairs={{0,32},{32,0},{64,96},{96,64},{128,160},{160,128},{192,224},{224,1... | collective-permute-start | bytes 786440 | tf_op jit(solution)/shard_map/ppermute | solution.py:24
  72.1 0.4 collective-permute-done.9.refs_6_
  72.5 2.4 %collective-permute-start.10 = (bf16[16,16,512]{2,1,0:T(8,128)(2,1)S(1)}, bf16[16,16,512]{2,1,0:T(8,128)(2,1)S(1)}, u32[]{:S(2)}, u32[]{:S(2)}) collective-permute-start(bf16[16,16,512]{2,1,0:T(8,128)(2,1)S(1)} %collective-permute-done.9.refs_6_), channel_id=1, source_target_pairs={{0,32},{32,0},{64,96},{96,64},{128,160},{160,128},{192,224},{224,1... | collective-permute-start | bytes 786440 | tf_op jit(solution)/shard_map/ppermute | solution.py:24
  74.9 2.7 %update.2 = (f32[8,64,512]{2,1,0:T(8,128)}, f32[8,64,512]{2,1,0:T(8,128)}, bf16[8,64,512]{2,1,0:T(8,128)(2,1)}) custom-call(bf16[16,16,512]{2,1,0:T(8,128)(2,1)S(1)} %get-tuple-element.24.refs_0_, bf16[16,16,512]{2,1,0:T(8,128)(2,1)S(1)} %collective-permute-done.11.refs_1_, bf16[16,16,512]{2,1,0:T(8,128)(2,1)S(1)} %collective-permute-done.12.refs_2_, ...), custom_call_target="tpu_custom_call" | custom-call | flops 536870912 | bytes 8388608 | tf_op jit(solution)/shard_map/update/pallas_call | solution.py:141
  77.7 2.7 %update.3 = (f32[8,64,512]{2,1,0:T(8,128)}, f32[8,64,512]{2,1,0:T(8,128)}, bf16[8,64,512]{2,1,0:T(8,128)(2,1)}) custom-call(bf16[16,16,512]{2,1,0:T(8,128)(2,1)S(1)} %get-tuple-element.22.refs_0_, bf16[16,16,512]{2,1,0:T(8,128)(2,1)S(1)} %collective-permute-done.4.refs_1_, ...), custom_call_target="tpu_custom_call", output_to_operand_aliasing={{0}: (12, {}), {1}: (13, {}), {2}: (14, {})} | custom-call | flops 536870912 | bytes 8388608 | tf_op jit(solution)/shard_map/update/pallas_call | solution.py:141
  (31 shorter events, 1.7 us)
Async XLA Ops:
  0.6 7.3 %collective-permute-start = (bf16[1,128,8192]{2,1,0:T(8,128)(2,1)}, bf16[1,128,8192]{2,1,0:T(8,128)(2,1)S(1)}, u32[]{:S(2)}, u32[]{:S(2)}) collective-permute-start(bf16[1,128,8192]{2,1,0:T(8,128)(2,1)} %param.6), channel_id=1, source_target_pairs={{0,32},{32,0},{64,96},{96,64},{128,160},{160,128},{192,224},{224,1... | collective-permute-start | bytes 6291464 | tf_op jit(solution)/shard_map/ppermute | solution.py:24
  4.0 1.6 %copy-start.4 = (bf16[1,128,8192]{2,1,0:T(8,128)(2,1)S(1)}, bf16[1,128,8192]{2,1,0:T(8,128)(2,1)}, u32[]{:S(2)}) copy-start(bf16[1,128,8192]{2,1,0:T(8,128)(2,1)} %param.6) | copy-start | bytes 6291460
  5.7 18.0 %copy-start.5 = (s32[8,16]{1,0:T(8,128)S(1)}, s32[8,16]{1,0:T(8,128)}, u32[]{:S(2)}) copy-start(s32[8,16]{1,0:T(8,128)} %table.1) | copy-start | bytes 1540
  8.0 67.0 %copy-start = (bf16[1,1,8,512,512]{4,3,2,1,0:T(8,128)(2,1)S(1)}, bf16[1,1,8,512,512]{4,3,2,1,0:T(8,128)(2,1)}, u32[]{:S(2)}) copy-start(bf16[1,1,8,512,512]{4,3,2,1,0:T(8,128)(2,1)} %param.10) | copy-start | bytes 12582916
  8.2 66.7 %copy-start.1 = (f32[1,1,8,64,512]{4,3,2,1,0:T(8,128)S(1)}, f32[1,1,8,64,512]{4,3,2,1,0:T(8,128)}, u32[]{:S(2)}) copy-start(f32[1,1,8,64,512]{4,3,2,1,0:T(8,128)} %param.7) | copy-start | bytes 3145732
  8.2 66.7 %copy-start.2 = (f32[1,1,8,64,512]{4,3,2,1,0:T(8,128)S(1)}, f32[1,1,8,64,512]{4,3,2,1,0:T(8,128)}, u32[]{:S(2)}) copy-start(f32[1,1,8,64,512]{4,3,2,1,0:T(8,128)} %param.8) | copy-start | bytes 3145732
  8.2 66.7 %copy-start.3 = (bf16[1,1,8,64,512]{4,3,2,1,0:T(8,128)(2,1)S(1)}, bf16[1,1,8,64,512]{4,3,2,1,0:T(8,128)(2,1)}, u32[]{:S(2)}) copy-start(bf16[1,1,8,64,512]{4,3,2,1,0:T(8,128)(2,1)} %param.9) | copy-start | bytes 1572868
  8.3 9.2 %collective-permute-start.1 = (bf16[16,8192]{1,0:T(8,128)(2,1)S(1)}, bf16[16,8192]{1,0:T(8,128)(2,1)S(1)}, u32[]{:S(2)}, u32[]{:S(2)}) collective-permute-start(bf16[16,8192]{1,0:T(8,128)(2,1)S(1)} %get-tuple-element.18), channel_id=1, source_target_pairs={{0,128},{32,160},{64,192},{96,224},{128,0},{160,32},{192,64},{224,... | collective-permute-start | bytes 786440 | tf_op jit(solution)/shard_map/ppermute | solution.py:24
  9.5 14.2 %collective-permute-start.2 = (bf16[16,8192]{1,0:T(8,128)(2,1)S(1)}, bf16[16,8192]{1,0:T(8,128)(2,1)S(1)}, u32[]{:S(2)}, u32[]{:S(2)}) collective-permute-start(bf16[16,8192]{1,0:T(8,128)(2,1)S(1)} %get-tuple-element.19), channel_id=1, source_target_pairs={{0,64},{32,96},{64,128},{96,160},{128,192},{160,224},{192,0},{224,... | collective-permute-start | bytes 786440 | tf_op jit(solution)/shard_map/ppermute | solution.py:24
  9.9 13.8 %collective-permute-start.3 = (bf16[16,8192]{1,0:T(8,128)(2,1)S(1)}, bf16[16,8192]{1,0:T(8,128)(2,1)S(1)}, u32[]{:S(2)}, u32[]{:S(2)}) collective-permute-start(bf16[16,8192]{1,0:T(8,128)(2,1)S(1)} %get-tuple-element.20), channel_id=1, source_target_pairs={{0,192},{32,224},{64,0},{96,32},{128,64},{160,96},{192,128},{224,1... | collective-permute-start | bytes 786440 | tf_op jit(solution)/shard_map/ppermute | solution.py:24
  47.6 5.3 %collective-permute-start.11 = (bf16[16,16,512]{2,1,0:T(8,128)(2,1)S(1)}, bf16[16,16,512]{2,1,0:T(8,128)(2,1)S(1)}, u32[]{:S(2)}, u32[]{:S(2)}) collective-permute-start(bf16[16,16,512]{2,1,0:T(8,128)(2,1)S(1)} %get-tuple-element.24.refs_0_), channel_id=1, source_target_pairs={{0,32},{32,0},{64,96},{96,64},{128,160},{160,128},{192,224},{224,1... | collective-permute-start | bytes 786440 | tf_op jit(solution)/shard_map/ppermute | solution.py:24
  51.7 3.4 %collective-permute-start.4 = (bf16[16,16,512]{2,1,0:T(8,128)(2,1)S(1)}, bf16[16,16,512]{2,1,0:T(8,128)(2,1)S(1)}, u32[]{:S(2)}, u32[]{:S(2)}) collective-permute-start(bf16[16,16,512]{2,1,0:T(8,128)(2,1)S(1)} %get-tuple-element.22.refs_0_), channel_id=1, source_target_pairs={{0,32},{32,0},{64,96},{96,64},{128,160},{160,128},{192,224},{224,1... | collective-permute-start | bytes 786440 | tf_op jit(solution)/shard_map/ppermute | solution.py:24
  52.9 5.6 %collective-permute-start.12 = (bf16[16,16,512]{2,1,0:T(8,128)(2,1)S(1)}, bf16[16,16,512]{2,1,0:T(8,128)(2,1)S(1)}, u32[]{:S(2)}, u32[]{:S(2)}) collective-permute-start(bf16[16,16,512]{2,1,0:T(8,128)(2,1)S(1)} %get-tuple-element.24.refs_0_), channel_id=1, source_target_pairs={{0,64},{32,224},{64,128},{96,32},{128,192},{160,96},{192,0},{224,1... | collective-permute-start | bytes 786440 | tf_op jit(solution)/shard_map/ppermute | solution.py:24
  55.2 6.5 %collective-permute-start.5 = (bf16[16,16,512]{2,1,0:T(8,128)(2,1)S(1)}, bf16[16,16,512]{2,1,0:T(8,128)(2,1)S(1)}, u32[]{:S(2)}, u32[]{:S(2)}) collective-permute-start(bf16[16,16,512]{2,1,0:T(8,128)(2,1)S(1)} %get-tuple-element.22.refs_0_), channel_id=1, source_target_pairs={{0,64},{32,224},{64,128},{96,32},{128,192},{160,96},{192,0},{224,1... | collective-permute-start | bytes 786440 | tf_op jit(solution)/shard_map/ppermute | solution.py:24
  55.6 8.9 %collective-permute-start.13 = (bf16[16,16,512]{2,1,0:T(8,128)(2,1)S(1)}, bf16[16,16,512]{2,1,0:T(8,128)(2,1)S(1)}, u32[]{:S(2)}, u32[]{:S(2)}) collective-permute-start(bf16[16,16,512]{2,1,0:T(8,128)(2,1)S(1)} %collective-permute-done.11.refs_1_), channel_id=1, source_target_pairs={{0,64},{32,224},{64,128},{96,32},{128,192},{160,96},{192,0},{224,1... | collective-permute-start | bytes 786440 | tf_op jit(solution)/shard_map/ppermute | solution.py:24
  58.5 8.4 %collective-permute-start.16 = (bf16[16,16,512]{2,1,0:T(8,128)(2,1)S(1)}, bf16[16,16,512]{2,1,0:T(8,128)(2,1)S(1)}, u32[]{:S(2)}, u32[]{:S(2)}) collective-permute-start(bf16[16,16,512]{2,1,0:T(8,128)(2,1)S(1)} %collective-permute-done.12.refs_2_), channel_id=1, source_target_pairs={{0,64},{32,224},{64,128},{96,32},{128,192},{160,96},{192,0},{224,1... | collective-permute-start | bytes 786440 | tf_op jit(solution)/shard_map/ppermute | solution.py:24
  61.6 8.1 %collective-permute-start.6 = (bf16[16,16,512]{2,1,0:T(8,128)(2,1)S(1)}, bf16[16,16,512]{2,1,0:T(8,128)(2,1)S(1)}, u32[]{:S(2)}, u32[]{:S(2)}) collective-permute-start(bf16[16,16,512]{2,1,0:T(8,128)(2,1)S(1)} %collective-permute-done.4.refs_1_), channel_id=1, source_target_pairs={{0,64},{32,224},{64,128},{96,32},{128,192},{160,96},{192,0},{224,1... | collective-permute-start | bytes 786440 | tf_op jit(solution)/shard_map/ppermute | solution.py:24
  61.6 10.4 %collective-permute-start.14 = (bf16[16,16,512]{2,1,0:T(8,128)(2,1)S(1)}, bf16[16,16,512]{2,1,0:T(8,128)(2,1)S(1)}, u32[]{:S(2)}, u32[]{:S(2)}) collective-permute-start(bf16[16,16,512]{2,1,0:T(8,128)(2,1)S(1)} %collective-permute-done.12.refs_2_), channel_id=1, source_target_pairs={{0,32},{32,0},{64,96},{96,64},{128,160},{160,128},{192,224},{224,1... | collective-permute-start | bytes 786440 | tf_op jit(solution)/shard_map/ppermute | solution.py:24
  61.7 10.9 %collective-permute-start.9 = (bf16[16,16,512]{2,1,0:T(8,128)(2,1)S(1)}, bf16[16,16,512]{2,1,0:T(8,128)(2,1)S(1)}, u32[]{:S(2)}, u32[]{:S(2)}) collective-permute-start(bf16[16,16,512]{2,1,0:T(8,128)(2,1)S(1)} %collective-permute-done.5.refs_2_), channel_id=1, source_target_pairs={{0,64},{32,224},{64,128},{96,32},{128,192},{160,96},{192,0},{224,1... | collective-permute-start | bytes 786440 | tf_op jit(solution)/shard_map/ppermute | solution.py:24
  64.4 10.5 %collective-permute-start.15 = (bf16[16,16,512]{2,1,0:T(8,128)(2,1)S(1)}, bf16[16,16,512]{2,1,0:T(8,128)(2,1)S(1)}, u32[]{:S(2)}, u32[]{:S(2)}) collective-permute-start(bf16[16,16,512]{2,1,0:T(8,128)(2,1)S(1)} %collective-permute-done.13.refs_3_), channel_id=1, source_target_pairs={{0,32},{32,0},{64,96},{96,64},{128,160},{160,128},{192,224},{224,1... | collective-permute-start | bytes 786440 | tf_op jit(solution)/shard_map/ppermute | solution.py:24
  66.9 8.0 %collective-permute-start.17 = (bf16[16,16,512]{2,1,0:T(8,128)(2,1)S(1)}, bf16[16,16,512]{2,1,0:T(8,128)(2,1)S(1)}, u32[]{:S(2)}, u32[]{:S(2)}) collective-permute-start(bf16[16,16,512]{2,1,0:T(8,128)(2,1)S(1)} %collective-permute-done.16.refs_6_), channel_id=1, source_target_pairs={{0,32},{32,0},{64,96},{96,64},{128,160},{160,128},{192,224},{224,1... | collective-permute-start | bytes 786440 | tf_op jit(solution)/shard_map/ppermute | solution.py:24
  69.7 7.9 %collective-permute-start.7 = (bf16[16,16,512]{2,1,0:T(8,128)(2,1)S(1)}, bf16[16,16,512]{2,1,0:T(8,128)(2,1)S(1)}, u32[]{:S(2)}, u32[]{:S(2)}) collective-permute-start(bf16[16,16,512]{2,1,0:T(8,128)(2,1)S(1)} %collective-permute-done.5.refs_2_), channel_id=1, source_target_pairs={{0,32},{32,0},{64,96},{96,64},{128,160},{160,128},{192,224},{224,1... | collective-permute-start | bytes 786440 | tf_op jit(solution)/shard_map/ppermute | solution.py:24
  72.1 5.5 %collective-permute-start.8 = (bf16[16,16,512]{2,1,0:T(8,128)(2,1)S(1)}, bf16[16,16,512]{2,1,0:T(8,128)(2,1)S(1)}, u32[]{:S(2)}, u32[]{:S(2)}) collective-permute-start(bf16[16,16,512]{2,1,0:T(8,128)(2,1)S(1)} %collective-permute-done.6.refs_3_), channel_id=1, source_target_pairs={{0,32},{32,0},{64,96},{96,64},{128,160},{160,128},{192,224},{224,1... | collective-permute-start | bytes 786440 | tf_op jit(solution)/shard_map/ppermute | solution.py:24
  72.5 5.1 %collective-permute-start.10 = (bf16[16,16,512]{2,1,0:T(8,128)(2,1)S(1)}, bf16[16,16,512]{2,1,0:T(8,128)(2,1)S(1)}, u32[]{:S(2)}, u32[]{:S(2)}) collective-permute-start(bf16[16,16,512]{2,1,0:T(8,128)(2,1)S(1)} %collective-permute-done.9.refs_6_), channel_id=1, source_target_pairs={{0,32},{32,0},{64,96},{96,64},{128,160},{160,128},{192,224},{224,1... | collective-permute-start | bytes 786440 | tf_op jit(solution)/shard_map/ppermute | solution.py:24

commit v3 on v2

--- a/solution.py
+++ b/solution.py
@@ -120,7 +120,7 @@
                 start = pl.multiple_of(q * quarter + row * 16, 16)
                 block[pl.ds(start, 16), :] = piece[4 * n + q]
         mine = block[pl.ds(pl.multiple_of(r * share, share), share), :]
-        stat_left = lax.dot_general(mine, block[...], (((1,), (1,)), ((), ())), preferred_element_type=jnp.float32)
+        stat_left = lax.dot_general(block[...], mine, (((1,), (1,)), ((), ())), preferred_element_type=jnp.float32).T
         left_new[n] = decay_rate * left[j] + scale * stat_left
         turned = block[:, pl.ds(pl.multiple_of(y * 2 * share, 2 * share), 2 * share)].T
         turned = jnp.where(core == 0, turned[:share], turned[share:])
@@ -162,13 +162,16 @@
 
 
 def gather(own, split):
-    parts = [own[: 4 * split], own[4 * split :]]
+    x, y = own[: 4 * split], own[4 * split :]
+    x_near = permute(x, split_ring)
+    x_other = cross(x)
+    y_tied, _ = tie(y, x_other)
+    y_other, y_near = cross(y_tied), permute(y_tied, split_ring)
+    x_near_other, y_near_other = permute(x_other, split_ring), permute(y_other, split_ring)
+    x_far, y_far = permute(tie(x_near, x_other, y_other)[0], split_ring), permute(tie(y_near, y_other)[0], split_ring)
     groups = []
-    for n, part in enumerate(parts):
-        a, b = tie(part, cross(part))
-        near, near_other = permute(a, split_ring), permute(b, split_ring)
-        far = permute(near, split_ring)
-        groups.append([part, b, near, near_other, cross(near), cross(near_other), far])
+    for part, other, near, near_other, far in ((x, x_other, x_near, x_near_other, x_far), (y, y_other, y_near, y_near_other, y_far)):
+        groups.append([part, other, near, near_other, cross(near), cross(near_other), far])
     return groups
 
 

time: 80.6 us -> 78.9 us (0.979)
  waiting for transfers between devices: 18.8 us -> 17.5 us
    ppermute x18, waiting for transfers between devices: 18.8 us -> 17.5 us  [permute(): return lax.ppermute(x, 'replica', pairs)]
  transfers between devices with their start and end apart: 18 -> 18, of which waited for: 8 -> 7; matrix products, arithmetic and copies ran while one was open for 0% -> 0% of each run, Pallas kernels for 3% -> 3%
where the time goes in v3:
time: 78.9 us; the launch traced here: 78.7 us
  starting transfers between devices  29.4 us (37%)
  blocking collectives  23.1 us (29%)
  waiting for transfers between devices  17.5 us (22%)
  Pallas kernels  6.15 us (8%)
  local copies, waits for them, and re-layouts  1.65 us (2%)
  between operations  0.92 us (1%)
    ppermute x18, starting transfers between devices, permute(): return lax.ppermute(x, 'replica', pairs)  29.4 us
    all_to_all x1, blocking collectives, shards(): lax.all_to_all(outgoing, 'fsdp', split_axis=0, concat_axis=0, tiled=True)  23.1 us
    ppermute x18, waiting for transfers between devices, permute(): return lax.ppermute(x, 'replica', pairs)  17.5 us
    pallas_call x2, Pallas kernels, update(): pl.pallas_call(lambda *refs: update_kernel(first, *refs), in_specs=[VMEM]...  5.02 us
    unnamed x12, local copies, waits for them, and re-layouts  1.62 us
  transfers between devices with their start and end apart: 18, of which 7 were waited for; matrix products, arithmetic and copies ran while one was open for 0% of the time, Pallas kernels for 3%

profile of v3, /device:TPU:1, one launch (start us, length us, event | category | flops | bytes accessed | tf_op | source)
XLA Modules:
  0.0 78.7 jit_solution(5604653021153278960)
XLA Ops:
  0.6 3.3 %collective-permute-start = (bf16[1,128,8192]{2,1,0:T(8,128)(2,1)}, bf16[1,128,8192]{2,1,0:T(8,128)(2,1)S(1)}, u32[]{:S(2)}, u32[]{:S(2)}) collective-permute-start(bf16[1,128,8192]{2,1,0:T(8,128)(2,1)} %param.6), channel_id=1, source_target_pairs={{0,32},{32,0},{64,96},{96,64},{128,160},{160,128},{192,224},{224,1... | collective-permute-start | bytes 6291464 | tf_op jit(solution)/shard_map/ppermute | solution.py:24
  4.0 1.6 %copy-done.4 = bf16[1,128,8192]{2,1,0:T(8,128)(2,1)S(1)} copy-done((bf16[1,128,8192]{2,1,0:T(8,128)(2,1)S(1)}, bf16[1,128,8192]{2,1,0:T(8,128)(2,1)}, u32[]{:S(2)}) %copy-start.4) | copy-done | bytes 2097176
  5.7 2.3 %collective-permute-done = bf16[1,128,8192]{2,1,0:T(8,128)(2,1)S(1)} collective-permute-done((bf16[1,128,8192]{2,1,0:T(8,128)(2,1)}, bf16[1,128,8192]{2,1,0:T(8,128)(2,1)S(1)}, u32[]{:S(2)}, u32[]{:S(2)}) %collective-permute-start) | collective-permute-done | bytes 2097184 | tf_op jit(solution)/shard_map/ppermute | solution.py:24
  8.3 1.3 %collective-permute-start.1 = (bf16[16,8192]{1,0:T(8,128)(2,1)S(1)}, bf16[16,8192]{1,0:T(8,128)(2,1)S(1)}, u32[]{:S(2)}, u32[]{:S(2)}) collective-permute-start(bf16[16,8192]{1,0:T(8,128)(2,1)S(1)} %get-tuple-element.17), channel_id=1, source_target_pairs={{0,128},{32,160},{64,192},{96,224},{128,0},{160,32},{192,64},{224,... | collective-permute-start | bytes 786440 | tf_op jit(solution)/shard_map/ppermute | solution.py:24
  9.9 2.3 %collective-permute-start.3 = (bf16[16,8192]{1,0:T(8,128)(2,1)S(1)}, bf16[16,8192]{1,0:T(8,128)(2,1)S(1)}, u32[]{:S(2)}, u32[]{:S(2)}) collective-permute-start(bf16[16,8192]{1,0:T(8,128)(2,1)S(1)} %get-tuple-element.19), channel_id=1, source_target_pairs={{0,192},{32,224},{64,0},{96,32},{128,64},{160,96},{192,128},{224,1... | collective-permute-start | bytes 786440 | tf_op jit(solution)/shard_map/ppermute | solution.py:24
  12.2 5.2 %collective-permute-done.1.refs_1_ = bf16[16,8192]{1,0:T(8,128)(2,1)S(1)} collective-permute-done((bf16[16,8192]{1,0:T(8,128)(2,1)S(1)}, bf16[16,8192]{1,0:T(8,128)(2,1)S(1)}, u32[]{:S(2)}, u32[]{:S(2)}) %collective-permute-start.1) | collective-permute-done | bytes 262176 | tf_op jit(solution)/shard_map/ppermute | solution.py:24
  17.4 6.3 %collective-permute-done.2.refs_2_ = bf16[16,8192]{1,0:T(8,128)(2,1)S(1)} collective-permute-done((bf16[16,8192]{1,0:T(8,128)(2,1)S(1)}, bf16[16,8192]{1,0:T(8,128)(2,1)S(1)}, u32[]{:S(2)}, u32[]{:S(2)}) %collective-permute-start.2) | collective-permute-done | bytes 262176 | tf_op jit(solution)/shard_map/ppermute | solution.py:24
  23.7 0.8 place.1
  24.5 23.1 %all_to_all.5 = bf16[32,16,512]{2,1,0:T(8,128)(2,1)S(1)} all-to-all(bf16[32,16,512]{2,1,0:T(8,128)(2,1)S(1)} %place.1), channel_id=1, replica_groups=mesh['replica'=8,'fsdp'=32] {'fsdp'}, dimensions={0} | all-to-all | bytes 1048576 | tf_op jit(solution)/shard_map/all_to_all | solution.py:193
  47.6 4.1 %collective-permute-start.4 = (bf16[16,16,512]{2,1,0:T(8,128)(2,1)S(1)}, bf16[16,16,512]{2,1,0:T(8,128)(2,1)S(1)}, u32[]{:S(2)}, u32[]{:S(2)}) collective-permute-start(bf16[16,16,512]{2,1,0:T(8,128)(2,1)S(1)} %get-tuple-element.29.refs_0_), channel_id=1, source_target_pairs={{0,32},{32,0},{64,96},{96,64},{128,160},{160,128},{192,224},{224,1... | collective-permute-start | bytes 786440 | tf_op jit(solution)/shard_map/ppermute | solution.py:24
  51.7 2.3 %collective-permute-start.12 = (bf16[16,16,512]{2,1,0:T(8,128)(2,1)S(1)}, bf16[16,16,512]{2,1,0:T(8,128)(2,1)S(1)}, u32[]{:S(2)}, u32[]{:S(2)}) collective-permute-start(bf16[16,16,512]{2,1,0:T(8,128)(2,1)S(1)} %get-tuple-element.29.refs_0_), channel_id=1, source_target_pairs={{0,64},{32,224},{64,128},{96,32},{128,192},{160,96},{192,0},{224,1... | collective-permute-start | bytes 786440 | tf_op jit(solution)/shard_map/ppermute | solution.py:24
  54.0 1.5 %collective-permute-start.6 = (bf16[16,16,512]{2,1,0:T(8,128)(2,1)S(1)}, bf16[16,16,512]{2,1,0:T(8,128)(2,1)S(1)}, u32[]{:S(2)}, u32[]{:S(2)}) collective-permute-start(bf16[16,16,512]{2,1,0:T(8,128)(2,1)S(1)} %get-tuple-element.20.refs_0_), channel_id=1, source_target_pairs={{0,64},{32,224},{64,128},{96,32},{128,192},{160,96},{192,0},{224,1... | collective-permute-start | bytes 786440 | tf_op jit(solution)/shard_map/ppermute | solution.py:24
  55.9 1.5 %collective-permute-done.12.refs_2_ = bf16[16,16,512]{2,1,0:T(8,128)(2,1)S(1)} collective-permute-done((bf16[16,16,512]{2,1,0:T(8,128)(2,1)S(1)}, bf16[16,16,512]{2,1,0:T(8,128)(2,1)S(1)}, u32[]{:S(2)}, u32[]{:S(2)}) %collective-permute-start.12) | collective-permute-done | bytes 262176 | tf_op jit(solution)/shard_map/ppermute | solution.py:24
  57.3 3.1 %collective-permute-start.16 = (bf16[16,16,512]{2,1,0:T(8,128)(2,1)S(1)}, bf16[16,16,512]{2,1,0:T(8,128)(2,1)S(1)}, u32[]{:S(2)}, u32[]{:S(2)}) collective-permute-start(bf16[16,16,512]{2,1,0:T(8,128)(2,1)S(1)} %collective-permute-done.12.refs_2_), channel_id=1, source_target_pairs={{0,64},{32,224},{64,128},{96,32},{128,192},{160,96},{192,0},{224,1... | collective-permute-start | bytes 786440 | tf_op jit(solution)/shard_map/ppermute | solution.py:24
  60.5 2.8 %collective-permute-start.10 = (bf16[16,16,512]{2,1,0:T(8,128)(2,1)S(1)}, bf16[16,16,512]{2,1,0:T(8,128)(2,1)S(1)}, u32[]{:S(2)}, u32[]{:S(2)}) collective-permute-start(bf16[16,16,512]{2,1,0:T(8,128)(2,1)S(1)} %collective-permute-done.6.refs_2_), channel_id=1, source_target_pairs={{0,64},{32,224},{64,128},{96,32},{128,192},{160,96},{192,0},{224,1... | collective-permute-start | bytes 786440 | tf_op jit(solution)/shard_map/ppermute | solution.py:24
  63.3 1.7 %collective-permute-start.15 = (bf16[16,16,512]{2,1,0:T(8,128)(2,1)S(1)}, bf16[16,16,512]{2,1,0:T(8,128)(2,1)S(1)}, u32[]{:S(2)}, u32[]{:S(2)}) collective-permute-start(bf16[16,16,512]{2,1,0:T(8,128)(2,1)S(1)} %collective-permute-done.13.refs_3_), channel_id=1, source_target_pairs={{0,32},{32,0},{64,96},{96,64},{128,160},{160,128},{192,224},{224,1... | collective-permute-start | bytes 786440 | tf_op jit(solution)/shard_map/ppermute | solution.py:24
  65.0 0.7 collective-permute-done.16.refs_6_
  65.8 2.1 %collective-permute-start.17 = (bf16[16,16,512]{2,1,0:T(8,128)(2,1)S(1)}, bf16[16,16,512]{2,1,0:T(8,128)(2,1)S(1)}, u32[]{:S(2)}, u32[]{:S(2)}) collective-permute-start(bf16[16,16,512]{2,1,0:T(8,128)(2,1)S(1)} %collective-permute-done.16.refs_6_), channel_id=1, source_target_pairs={{0,32},{32,0},{64,96},{96,64},{128,160},{160,128},{192,224},{224,1... | collective-permute-start | bytes 786440 | tf_op jit(solution)/shard_map/ppermute | solution.py:24
  67.8 0.7 collective-permute-done.10.refs_6_
  68.6 2.1 %collective-permute-start.11 = (bf16[16,16,512]{2,1,0:T(8,128)(2,1)S(1)}, bf16[16,16,512]{2,1,0:T(8,128)(2,1)S(1)}, u32[]{:S(2)}, u32[]{:S(2)}) collective-permute-start(bf16[16,16,512]{2,1,0:T(8,128)(2,1)S(1)} %collective-permute-done.10.refs_6_), channel_id=1, source_target_pairs={{0,32},{32,0},{64,96},{96,64},{128,160},{160,128},{192,224},{224,1... | collective-permute-start | bytes 786440 | tf_op jit(solution)/shard_map/ppermute | solution.py:24
  70.6 0.7 collective-permute-done.7.refs_3_
  71.4 2.1 %collective-permute-start.9 = (bf16[16,16,512]{2,1,0:T(8,128)(2,1)S(1)}, bf16[16,16,512]{2,1,0:T(8,128)(2,1)S(1)}, u32[]{:S(2)}, u32[]{:S(2)}) collective-permute-start(bf16[16,16,512]{2,1,0:T(8,128)(2,1)S(1)} %collective-permute-done.7.refs_3_), channel_id=1, source_target_pairs={{0,32},{32,0},{64,96},{96,64},{128,160},{160,128},{192,224},{224,1... | collective-permute-start | bytes 786440 | tf_op jit(solution)/shard_map/ppermute | solution.py:24
  73.5 2.5 %update.2 = (f32[8,64,512]{2,1,0:T(8,128)}, f32[8,64,512]{2,1,0:T(8,128)}, bf16[8,64,512]{2,1,0:T(8,128)(2,1)}) custom-call(bf16[16,16,512]{2,1,0:T(8,128)(2,1)S(1)} %get-tuple-element.29.refs_0_, bf16[16,16,512]{2,1,0:T(8,128)(2,1)S(1)} %collective-permute-done.4.refs_1_, bf16[16,16,512]{2,1,0:T(8,128)(2,1)S(1)} %collective-permute-done.12.refs_2_, ...), custom_call_target="tpu_custom_call" | custom-call | flops 536870912 | bytes 8388608 | tf_op jit(solution)/shard_map/update/pallas_call | solution.py:141
  76.0 2.5 %update.3 = (f32[8,64,512]{2,1,0:T(8,128)}, f32[8,64,512]{2,1,0:T(8,128)}, bf16[8,64,512]{2,1,0:T(8,128)(2,1)}) custom-call(bf16[16,16,512]{2,1,0:T(8,128)(2,1)S(1)} %get-tuple-element.20.refs_0_, bf16[16,16,512]{2,1,0:T(8,128)(2,1)S(1)} %collective-permute-done.5.refs_1_, ...), custom_call_target="tpu_custom_call", output_to_operand_aliasing={{0}: (12, {}), {1}: (13, {}), {2}: (14, {})} | custom-call | flops 536870912 | bytes 8388608 | tf_op jit(solution)/shard_map/update/pallas_call | solution.py:141
  (31 shorter events, 1.2 us)
Async XLA Ops:
  0.6 7.3 %collective-permute-start = (bf16[1,128,8192]{2,1,0:T(8,128)(2,1)}, bf16[1,128,8192]{2,1,0:T(8,128)(2,1)S(1)}, u32[]{:S(2)}, u32[]{:S(2)}) collective-permute-start(bf16[1,128,8192]{2,1,0:T(8,128)(2,1)} %param.6), channel_id=1, source_target_pairs={{0,32},{32,0},{64,96},{96,64},{128,160},{160,128},{192,224},{224,1... | collective-permute-start | bytes 6291464 | tf_op jit(solution)/shard_map/ppermute | solution.py:24
  4.0 1.6 %copy-start.4 = (bf16[1,128,8192]{2,1,0:T(8,128)(2,1)S(1)}, bf16[1,128,8192]{2,1,0:T(8,128)(2,1)}, u32[]{:S(2)}) copy-start(bf16[1,128,8192]{2,1,0:T(8,128)(2,1)} %param.6) | copy-start | bytes 6291460
  5.7 18.0 %copy-start.5 = (s32[8,16]{1,0:T(8,128)S(1)}, s32[8,16]{1,0:T(8,128)}, u32[]{:S(2)}) copy-start(s32[8,16]{1,0:T(8,128)} %table.1) | copy-start | bytes 1540
  8.0 65.5 %copy-start = (bf16[1,1,8,512,512]{4,3,2,1,0:T(8,128)(2,1)S(1)}, bf16[1,1,8,512,512]{4,3,2,1,0:T(8,128)(2,1)}, u32[]{:S(2)}) copy-start(bf16[1,1,8,512,512]{4,3,2,1,0:T(8,128)(2,1)} %param.10) | copy-start | bytes 12582916
  8.2 65.2 %copy-start.1 = (f32[1,1,8,64,512]{4,3,2,1,0:T(8,128)S(1)}, f32[1,1,8,64,512]{4,3,2,1,0:T(8,128)}, u32[]{:S(2)}) copy-start(f32[1,1,8,64,512]{4,3,2,1,0:T(8,128)} %param.7) | copy-start | bytes 3145732
  8.2 65.2 %copy-start.2 = (f32[1,1,8,64,512]{4,3,2,1,0:T(8,128)S(1)}, f32[1,1,8,64,512]{4,3,2,1,0:T(8,128)}, u32[]{:S(2)}) copy-start(f32[1,1,8,64,512]{4,3,2,1,0:T(8,128)} %param.8) | copy-start | bytes 3145732
  8.2 65.2 %copy-start.3 = (bf16[1,1,8,64,512]{4,3,2,1,0:T(8,128)(2,1)S(1)}, bf16[1,1,8,64,512]{4,3,2,1,0:T(8,128)(2,1)}, u32[]{:S(2)}) copy-start(bf16[1,1,8,64,512]{4,3,2,1,0:T(8,128)(2,1)} %param.9) | copy-start | bytes 1572868
  8.3 9.2 %collective-permute-start.1 = (bf16[16,8192]{1,0:T(8,128)(2,1)S(1)}, bf16[16,8192]{1,0:T(8,128)(2,1)S(1)}, u32[]{:S(2)}, u32[]{:S(2)}) collective-permute-start(bf16[16,8192]{1,0:T(8,128)(2,1)S(1)} %get-tuple-element.17), channel_id=1, source_target_pairs={{0,128},{32,160},{64,192},{96,224},{128,0},{160,32},{192,64},{224,... | collective-permute-start | bytes 786440 | tf_op jit(solution)/shard_map/ppermute | solution.py:24
  9.5 14.2 %collective-permute-start.2 = (bf16[16,8192]{1,0:T(8,128)(2,1)S(1)}, bf16[16,8192]{1,0:T(8,128)(2,1)S(1)}, u32[]{:S(2)}, u32[]{:S(2)}) collective-permute-start(bf16[16,8192]{1,0:T(8,128)(2,1)S(1)} %get-tuple-element.18), channel_id=1, source_target_pairs={{0,64},{32,96},{64,128},{96,160},{128,192},{160,224},{192,0},{224,... | collective-permute-start | bytes 786440 | tf_op jit(solution)/shard_map/ppermute | solution.py:24
  9.9 13.8 %collective-permute-start.3 = (bf16[16,8192]{1,0:T(8,128)(2,1)S(1)}, bf16[16,8192]{1,0:T(8,128)(2,1)S(1)}, u32[]{:S(2)}, u32[]{:S(2)}) collective-permute-start(bf16[16,8192]{1,0:T(8,128)(2,1)S(1)} %get-tuple-element.19), channel_id=1, source_target_pairs={{0,192},{32,224},{64,0},{96,32},{128,64},{160,96},{192,128},{224,1... | collective-permute-start | bytes 786440 | tf_op jit(solution)/shard_map/ppermute | solution.py:24
  47.6 6.4 %collective-permute-start.4 = (bf16[16,16,512]{2,1,0:T(8,128)(2,1)S(1)}, bf16[16,16,512]{2,1,0:T(8,128)(2,1)S(1)}, u32[]{:S(2)}, u32[]{:S(2)}) collective-permute-start(bf16[16,16,512]{2,1,0:T(8,128)(2,1)S(1)} %get-tuple-element.29.refs_0_), channel_id=1, source_target_pairs={{0,32},{32,0},{64,96},{96,64},{128,160},{160,128},{192,224},{224,1... | collective-permute-start | bytes 786440 | tf_op jit(solution)/shard_map/ppermute | solution.py:24
  51.7 5.6 %collective-permute-start.12 = (bf16[16,16,512]{2,1,0:T(8,128)(2,1)S(1)}, bf16[16,16,512]{2,1,0:T(8,128)(2,1)S(1)}, u32[]{:S(2)}, u32[]{:S(2)}) collective-permute-start(bf16[16,16,512]{2,1,0:T(8,128)(2,1)S(1)} %get-tuple-element.29.refs_0_), channel_id=1, source_target_pairs={{0,64},{32,224},{64,128},{96,32},{128,192},{160,96},{192,0},{224,1... | collective-permute-start | bytes 786440 | tf_op jit(solution)/shard_map/ppermute | solution.py:24
  54.0 3.3 %collective-permute-start.5 = (bf16[16,16,512]{2,1,0:T(8,128)(2,1)S(1)}, bf16[16,16,512]{2,1,0:T(8,128)(2,1)S(1)}, u32[]{:S(2)}, u32[]{:S(2)}) collective-permute-start(bf16[16,16,512]{2,1,0:T(8,128)(2,1)S(1)} %get-tuple-element.20.refs_0_), channel_id=1, source_target_pairs={{0,32},{32,0},{64,96},{96,64},{128,160},{160,128},{192,224},{224,1... | collective-permute-start | bytes 786440 | tf_op jit(solution)/shard_map/ppermute | solution.py:24
  54.0 6.4 %collective-permute-start.6 = (bf16[16,16,512]{2,1,0:T(8,128)(2,1)S(1)}, bf16[16,16,512]{2,1,0:T(8,128)(2,1)S(1)}, u32[]{:S(2)}, u32[]{:S(2)}) collective-permute-start(bf16[16,16,512]{2,1,0:T(8,128)(2,1)S(1)} %get-tuple-element.20.refs_0_), channel_id=1, source_target_pairs={{0,64},{32,224},{64,128},{96,32},{128,192},{160,96},{192,0},{224,1... | collective-permute-start | bytes 786440 | tf_op jit(solution)/shard_map/ppermute | solution.py:24
  55.6 7.7 %collective-permute-start.13 = (bf16[16,16,512]{2,1,0:T(8,128)(2,1)S(1)}, bf16[16,16,512]{2,1,0:T(8,128)(2,1)S(1)}, u32[]{:S(2)}, u32[]{:S(2)}) collective-permute-start(bf16[16,16,512]{2,1,0:T(8,128)(2,1)S(1)} %collective-permute-done.4.refs_1_), channel_id=1, source_target_pairs={{0,64},{32,224},{64,128},{96,32},{128,192},{160,96},{192,0},{224,1... | collective-permute-start | bytes 786440 | tf_op jit(solution)/shard_map/ppermute | solution.py:24
  57.3 8.4 %collective-permute-start.16 = (bf16[16,16,512]{2,1,0:T(8,128)(2,1)S(1)}, bf16[16,16,512]{2,1,0:T(8,128)(2,1)S(1)}, u32[]{:S(2)}, u32[]{:S(2)}) collective-permute-start(bf16[16,16,512]{2,1,0:T(8,128)(2,1)S(1)} %collective-permute-done.12.refs_2_), channel_id=1, source_target_pairs={{0,64},{32,224},{64,128},{96,32},{128,192},{160,96},{192,0},{224,1... | collective-permute-start | bytes 786440 | tf_op jit(solution)/shard_map/ppermute | solution.py:24
  60.5 7.4 %collective-permute-start.14 = (bf16[16,16,512]{2,1,0:T(8,128)(2,1)S(1)}, bf16[16,16,512]{2,1,0:T(8,128)(2,1)S(1)}, u32[]{:S(2)}, u32[]{:S(2)}) collective-permute-start(bf16[16,16,512]{2,1,0:T(8,128)(2,1)S(1)} %collective-permute-done.12.refs_2_), channel_id=1, source_target_pairs={{0,32},{32,0},{64,96},{96,64},{128,160},{160,128},{192,224},{224,1... | collective-permute-start | bytes 786440 | tf_op jit(solution)/shard_map/ppermute | solution.py:24
  60.5 8.1 %collective-permute-start.10 = (bf16[16,16,512]{2,1,0:T(8,128)(2,1)S(1)}, bf16[16,16,512]{2,1,0:T(8,128)(2,1)S(1)}, u32[]{:S(2)}, u32[]{:S(2)}) collective-permute-start(bf16[16,16,512]{2,1,0:T(8,128)(2,1)S(1)} %collective-permute-done.6.refs_2_), channel_id=1, source_target_pairs={{0,64},{32,224},{64,128},{96,32},{128,192},{160,96},{192,0},{224,1... | collective-permute-start | bytes 786440 | tf_op jit(solution)/shard_map/ppermute | solution.py:24
  63.3 8.1 %collective-permute-start.7 = (bf16[16,16,512]{2,1,0:T(8,128)(2,1)S(1)}, bf16[16,16,512]{2,1,0:T(8,128)(2,1)S(1)}, u32[]{:S(2)}, u32[]{:S(2)}) collective-permute-start(bf16[16,16,512]{2,1,0:T(8,128)(2,1)S(1)} %collective-permute-done.5.refs_1_), channel_id=1, source_target_pairs={{0,64},{32,224},{64,128},{96,32},{128,192},{160,96},{192,0},{224,1... | collective-permute-start | bytes 786440 | tf_op jit(solution)/shard_map/ppermute | solution.py:24
  63.3 10.2 %collective-permute-start.15 = (bf16[16,16,512]{2,1,0:T(8,128)(2,1)S(1)}, bf16[16,16,512]{2,1,0:T(8,128)(2,1)S(1)}, u32[]{:S(2)}, u32[]{:S(2)}) collective-permute-start(bf16[16,16,512]{2,1,0:T(8,128)(2,1)S(1)} %collective-permute-done.13.refs_3_), channel_id=1, source_target_pairs={{0,32},{32,0},{64,96},{96,64},{128,160},{160,128},{192,224},{224,1... | collective-permute-start | bytes 786440 | tf_op jit(solution)/shard_map/ppermute | solution.py:24
  65.8 7.7 %collective-permute-start.17 = (bf16[16,16,512]{2,1,0:T(8,128)(2,1)S(1)}, bf16[16,16,512]{2,1,0:T(8,128)(2,1)S(1)}, u32[]{:S(2)}, u32[]{:S(2)}) collective-permute-start(bf16[16,16,512]{2,1,0:T(8,128)(2,1)S(1)} %collective-permute-done.16.refs_6_), channel_id=1, source_target_pairs={{0,32},{32,0},{64,96},{96,64},{128,160},{160,128},{192,224},{224,1... | collective-permute-start | bytes 786440 | tf_op jit(solution)/shard_map/ppermute | solution.py:24
  67.8 8.2 %collective-permute-start.8 = (bf16[16,16,512]{2,1,0:T(8,128)(2,1)S(1)}, bf16[16,16,512]{2,1,0:T(8,128)(2,1)S(1)}, u32[]{:S(2)}, u32[]{:S(2)}) collective-permute-start(bf16[16,16,512]{2,1,0:T(8,128)(2,1)S(1)} %collective-permute-done.6.refs_2_), channel_id=1, source_target_pairs={{0,32},{32,0},{64,96},{96,64},{128,160},{160,128},{192,224},{224,1... | collective-permute-start | bytes 786440 | tf_op jit(solution)/shard_map/ppermute | solution.py:24
  68.6 7.5 %collective-permute-start.11 = (bf16[16,16,512]{2,1,0:T(8,128)(2,1)S(1)}, bf16[16,16,512]{2,1,0:T(8,128)(2,1)S(1)}, u32[]{:S(2)}, u32[]{:S(2)}) collective-permute-start(bf16[16,16,512]{2,1,0:T(8,128)(2,1)S(1)} %collective-permute-done.10.refs_6_), channel_id=1, source_target_pairs={{0,32},{32,0},{64,96},{96,64},{128,160},{160,128},{192,224},{224,1... | collective-permute-start | bytes 786440 | tf_op jit(solution)/shard_map/ppermute | solution.py:24
  71.4 4.7 %collective-permute-start.9 = (bf16[16,16,512]{2,1,0:T(8,128)(2,1)S(1)}, bf16[16,16,512]{2,1,0:T(8,128)(2,1)S(1)}, u32[]{:S(2)}, u32[]{:S(2)}) collective-permute-start(bf16[16,16,512]{2,1,0:T(8,128)(2,1)S(1)} %collective-permute-done.7.refs_3_), channel_id=1, source_target_pairs={{0,32},{32,0},{64,96},{96,64},{128,160},{160,128},{192,224},{224,1... | collective-permute-start | bytes 786440 | tf_op jit(solution)/shard_map/ppermute | solution.py:24

commit v4 on v3

--- a/solution.py
+++ b/solution.py
@@ -28,45 +28,52 @@
     return 2 * lax.rem(r // 2 + k, 4) + lax.rem(r, 2)
 
 
-def own_rows_kernel(grads, out, sems):
-    copies = [pltpu.make_async_copy(grads.at[group_of(lax.axis_index("replica"), k)], out.at[k], sems.at[k]) for k in range(4)]
+def split_kernel(grads, own, first, second, sems):
+    r = lax.axis_index("replica")
+    copies = []
+    for k in range(4):
+        target = (second, first, first, second)[k]
+        slot = (1, 1, 0, 0)[k]
+        mine = group_of(r, k)
+        theirs = mine + 1 - 2 * lax.rem(r, 2)
+        copies.append(pltpu.make_async_copy(grads.at[theirs], target.at[slot], sems.at[2 * k]))
+        copies.append(pltpu.make_async_copy(grads.at[mine], own.at[k], sems.at[2 * k + 1]))
     for c in copies:
         c.start()
     for c in copies:
         c.wait()
 
 
-def own_rows(grads):
+def split(grads):
     _, rows, cols = grads.shape
     return pl.pallas_call(
-        own_rows_kernel,
+        split_kernel,
         in_specs=[HBM],
-        out_specs=VMEM,
-        out_shape=jax.ShapeDtypeStruct((4, rows, cols), grads.dtype),
-        scratch_shapes=[pltpu.SemaphoreType.DMA((4,))],
+        out_specs=[VMEM] * 3,
+        out_shape=[jax.ShapeDtypeStruct((n, rows, cols), grads.dtype) for n in (4, 2, 2)],
+        scratch_shapes=[pltpu.SemaphoreType.DMA((8,))],
         compiler_params=pltpu.CompilerParams(vmem_limit_bytes=8 * MIB),
         cost_estimate=pl.CostEstimate(flops=0, bytes_accessed=4 * MIB, transcendentals=0),
-        name="own_rows",
+        name="split",
     )(grads)
 
 
-def pair_sum_kernel(own, recv, *outs):
-    for k in range(4):
-        total = own[k].astype(jnp.float32) + recv[group_of(lax.axis_index("replica"), k)].astype(jnp.float32)
-        outs[k][...] = total.astype(own.dtype)
-
-
-def pair_sum(own, recv, block):
+def pair_sum_kernel(groups, own, recv, *outs):
+    for n, k in enumerate(groups):
+        outs[n][...] = (own[k].astype(jnp.float32) + recv[n].astype(jnp.float32)).astype(own.dtype)
+
+
+def pair_sum(groups, own, recv, *extra):
     _, rows, cols = own.shape
     return pl.pallas_call(
-        pair_sum_kernel,
-        in_specs=[VMEM, VMEM],
-        out_specs=[VMEM] * 4,
-        out_shape=[jax.ShapeDtypeStruct((rows, cols), own.dtype)] * 4,
+        lambda own, recv, *refs: pair_sum_kernel(groups, own, recv, *refs[-2:]),
+        in_specs=[VMEM, VMEM] + [SMEM] * len(extra),
+        out_specs=[VMEM] * 2,
+        out_shape=[jax.ShapeDtypeStruct((rows, cols), own.dtype)] * 2,
         compiler_params=pltpu.CompilerParams(vmem_limit_bytes=8 * MIB),
-        cost_estimate=pl.CostEstimate(flops=4 * rows * cols, bytes_accessed=4 * MIB, transcendentals=0),
+        cost_estimate=pl.CostEstimate(flops=2 * rows * cols, bytes_accessed=2 * MIB, transcendentals=0),
         name="pair_sum",
-    )(own, recv)
+    )(own, recv, *extra)
 
 
 def place_kernel(table, *refs):
@@ -183,11 +190,11 @@
     block = left_factor.shape[-1]
     _, row_count, col_count = gradients.shape
 
-    swapped = permute(gradients, core_swap)
-    grouped = (8, row_count // 8, col_count)
-    own = own_rows(gradients.reshape(grouped))
-    sums = pair_sum(own, swapped.reshape(grouped), block)
-    kept, to_next, to_far, to_prev = sums
+    own, first, second = split(gradients.reshape(8, row_count // 8, col_count))
+    first = cross(first)
+    to_far, to_next = pair_sum((2, 1), own, first)
+    second, _ = tie(second, first)
+    to_prev, kept = pair_sum((3, 0), own, cross(second), owner_table)
     parts = [kept, permute(to_far, y_shift(2)), permute(to_next, y_shift(1)), permute(to_prev, y_shift(-1))]
     (outgoing,) = place(owner_table, parts, owners, block)
     received = lax.all_to_all(outgoing, "fsdp", split_axis=0, concat_axis=0, tiled=True)

time: 78.9 us -> 78.4 us (level)
  waiting for transfers between devices: 17.5 us -> 15.5 us
    ppermute x18 -> x19, waiting for transfers between devices: 17.5 us -> 15.5 us  [permute(): return lax.ppermute(x, 'replica', pairs)]
    ppermute x18 -> x19, starting transfers between devices: 29.4 us -> 29.5 us  [permute(): return lax.ppermute(x, 'replica', pairs)]
  transfers between devices with their start and end apart: 18 -> 19, of which waited for: 7 -> 7; matrix products, arithmetic and copies ran while one was open for 0% -> 0% of each run, Pallas kernels for 3% -> 4%
where the time goes in v4:
time: 78.4 us; the launch traced here: 78.2 us
  starting transfers between devices  29.5 us (38%)
  blocking collectives  23.1 us (29%)
  waiting for transfers between devices  15.5 us (20%)
  Pallas kernels  6.87 us (9%)
  local copies, waits for them, and re-layouts  2.32 us (3%)
  between operations  0.91 us (1%)
    ppermute x19, starting transfers between devices, permute(): return lax.ppermute(x, 'replica', pairs)  29.5 us
    all_to_all x1, blocking collectives, shards(): lax.all_to_all(outgoing, 'fsdp', split_axis=0, concat_axis=0, tiled=True)  23.1 us
    ppermute x19, waiting for transfers between devices, permute(): return lax.ppermute(x, 'replica', pairs)  15.5 us
    pallas_call x2, Pallas kernels, update(): pl.pallas_call(lambda *refs: update_kernel(first, *refs), in_specs=[VMEM]...  5.02 us
    unnamed x12, local copies, waits for them, and re-layouts  2.29 us
  transfers between devices with their start and end apart: 19, of which 7 were waited for; matrix products, arithmetic and copies ran while one was open for 0% of the time, Pallas kernels for 4%

profile of v4, /device:TPU:1, one launch (start us, length us, event | category | flops | bytes accessed | tf_op | source)
XLA Modules:
  0.0 78.2 jit_solution(861199717519424644)
XLA Ops:
  0.6 1.6 %copy-done.4 = bf16[1,128,8192]{2,1,0:T(8,128)(2,1)S(1)} copy-done((bf16[1,128,8192]{2,1,0:T(8,128)(2,1)S(1)}, bf16[1,128,8192]{2,1,0:T(8,128)(2,1)}, u32[]{:S(2)}) %copy-start.4) | copy-done | bytes 2097176
  2.5 3.3 %collective-permute-start = (bf16[2,16,8192]{2,1,0:T(8,128)(2,1)S(1)}, bf16[2,16,8192]{2,1,0:T(8,128)(2,1)S(1)}, u32[]{:S(2)}, u32[]{:S(2)}) collective-permute-start(bf16[2,16,8192]{2,1,0:T(8,128)(2,1)S(1)} %get-tuple-element.22), channel_id=1, source_target_pairs={{0,32},{32,0},{64,96},{96,64},{128,160},{160,128},{192,224},{224,1... | collective-permute-start | bytes 1572872 | tf_op jit(solution)/shard_map/ppermute | solution.py:24
  5.8 1.5 %collective-permute-done.recv = bf16[2,16,8192]{2,1,0:T(8,128)(2,1)S(1)} collective-permute-done((bf16[2,16,8192]{2,1,0:T(8,128)(2,1)S(1)}, bf16[2,16,8192]{2,1,0:T(8,128)(2,1)S(1)}, u32[]{:S(2)}, u32[]{:S(2)}) %collective-permute-start) | collective-permute-done | bytes 524320 | tf_op jit(solution)/shard_map/ppermute | solution.py:24
  7.9 1.3 %collective-permute-start.2 = (bf16[16,8192]{1,0:T(8,128)(2,1)S(1)}, bf16[16,8192]{1,0:T(8,128)(2,1)S(1)}, u32[]{:S(2)}, u32[]{:S(2)}) collective-permute-start(bf16[16,8192]{1,0:T(8,128)(2,1)S(1)} %get-tuple-element.25), channel_id=1, source_target_pairs={{0,128},{32,160},{64,192},{96,224},{128,0},{160,32},{192,64},{224,... | collective-permute-start | bytes 786440 | tf_op jit(solution)/shard_map/ppermute | solution.py:24
  11.0 2.4 %collective-permute-start.4 = (bf16[16,8192]{1,0:T(8,128)(2,1)S(1)}, bf16[16,8192]{1,0:T(8,128)(2,1)S(1)}, u32[]{:S(2)}, u32[]{:S(2)}) collective-permute-start(bf16[16,8192]{1,0:T(8,128)(2,1)S(1)} %get-tuple-element.27), channel_id=1, source_target_pairs={{0,192},{32,224},{64,0},{96,32},{128,64},{160,96},{192,128},{224,1... | collective-permute-start | bytes 786440 | tf_op jit(solution)/shard_map/ppermute | solution.py:24
  13.3 4.0 %collective-permute-done.2.refs_1_ = bf16[16,8192]{1,0:T(8,128)(2,1)S(1)} collective-permute-done((bf16[16,8192]{1,0:T(8,128)(2,1)S(1)}, bf16[16,8192]{1,0:T(8,128)(2,1)S(1)}, u32[]{:S(2)}, u32[]{:S(2)}) %collective-permute-start.2) | collective-permute-done | bytes 262176 | tf_op jit(solution)/shard_map/ppermute | solution.py:24
  17.3 6.0 %collective-permute-done.3.refs_2_ = bf16[16,8192]{1,0:T(8,128)(2,1)S(1)} collective-permute-done((bf16[16,8192]{1,0:T(8,128)(2,1)S(1)}, bf16[16,8192]{1,0:T(8,128)(2,1)S(1)}, u32[]{:S(2)}, u32[]{:S(2)}) %collective-permute-start.3) | collective-permute-done | bytes 262176 | tf_op jit(solution)/shard_map/ppermute | solution.py:24
  23.3 0.8 place.1
  24.1 23.1 %all_to_all.5 = bf16[32,16,512]{2,1,0:T(8,128)(2,1)S(1)} all-to-all(bf16[32,16,512]{2,1,0:T(8,128)(2,1)S(1)} %place.1), channel_id=1, replica_groups=mesh['replica'=8,'fsdp'=32] {'fsdp'}, dimensions={0} | all-to-all | bytes 1048576 | tf_op jit(solution)/shard_map/all_to_all | solution.py:200
  47.2 4.0 %collective-permute-start.5 = (bf16[16,16,512]{2,1,0:T(8,128)(2,1)S(1)}, bf16[16,16,512]{2,1,0:T(8,128)(2,1)S(1)}, u32[]{:S(2)}, u32[]{:S(2)}) collective-permute-start(bf16[16,16,512]{2,1,0:T(8,128)(2,1)S(1)} %get-tuple-element.37.refs_0_), channel_id=1, source_target_pairs={{0,32},{32,0},{64,96},{96,64},{128,160},{160,128},{192,224},{224,1... | collective-permute-start | bytes 786440 | tf_op jit(solution)/shard_map/ppermute | solution.py:24
  51.2 2.4 %collective-permute-start.13 = (bf16[16,16,512]{2,1,0:T(8,128)(2,1)S(1)}, bf16[16,16,512]{2,1,0:T(8,128)(2,1)S(1)}, u32[]{:S(2)}, u32[]{:S(2)}) collective-permute-start(bf16[16,16,512]{2,1,0:T(8,128)(2,1)S(1)} %get-tuple-element.37.refs_0_), channel_id=1, source_target_pairs={{0,64},{32,224},{64,128},{96,32},{128,192},{160,96},{192,0},{224,1... | collective-permute-start | bytes 786440 | tf_op jit(solution)/shard_map/ppermute | solution.py:24
  53.6 1.5 %collective-permute-start.7 = (bf16[16,16,512]{2,1,0:T(8,128)(2,1)S(1)}, bf16[16,16,512]{2,1,0:T(8,128)(2,1)S(1)}, u32[]{:S(2)}, u32[]{:S(2)}) collective-permute-start(bf16[16,16,512]{2,1,0:T(8,128)(2,1)S(1)} %get-tuple-element.28.refs_0_), channel_id=1, source_target_pairs={{0,64},{32,224},{64,128},{96,32},{128,192},{160,96},{192,0},{224,1... | collective-permute-start | bytes 786440 | tf_op jit(solution)/shard_map/ppermute | solution.py:24
  55.5 1.5 %collective-permute-done.13.refs_2_ = bf16[16,16,512]{2,1,0:T(8,128)(2,1)S(1)} collective-permute-done((bf16[16,16,512]{2,1,0:T(8,128)(2,1)S(1)}, bf16[16,16,512]{2,1,0:T(8,128)(2,1)S(1)}, u32[]{:S(2)}, u32[]{:S(2)}) %collective-permute-start.13) | collective-permute-done | bytes 262176 | tf_op jit(solution)/shard_map/ppermute | solution.py:24
  56.9 3.1 %collective-permute-start.17 = (bf16[16,16,512]{2,1,0:T(8,128)(2,1)S(1)}, bf16[16,16,512]{2,1,0:T(8,128)(2,1)S(1)}, u32[]{:S(2)}, u32[]{:S(2)}) collective-permute-start(bf16[16,16,512]{2,1,0:T(8,128)(2,1)S(1)} %collective-permute-done.13.refs_2_), channel_id=1, source_target_pairs={{0,64},{32,224},{64,128},{96,32},{128,192},{160,96},{192,0},{224,1... | collective-permute-start | bytes 786440 | tf_op jit(solution)/shard_map/ppermute | solution.py:24
  60.1 2.8 %collective-permute-start.11 = (bf16[16,16,512]{2,1,0:T(8,128)(2,1)S(1)}, bf16[16,16,512]{2,1,0:T(8,128)(2,1)S(1)}, u32[]{:S(2)}, u32[]{:S(2)}) collective-permute-start(bf16[16,16,512]{2,1,0:T(8,128)(2,1)S(1)} %collective-permute-done.7.refs_2_), channel_id=1, source_target_pairs={{0,64},{32,224},{64,128},{96,32},{128,192},{160,96},{192,0},{224,1... | collective-permute-start | bytes 786440 | tf_op jit(solution)/shard_map/ppermute | solution.py:24
  62.9 1.6 %collective-permute-start.16 = (bf16[16,16,512]{2,1,0:T(8,128)(2,1)S(1)}, bf16[16,16,512]{2,1,0:T(8,128)(2,1)S(1)}, u32[]{:S(2)}, u32[]{:S(2)}) collective-permute-start(bf16[16,16,512]{2,1,0:T(8,128)(2,1)S(1)} %collective-permute-done.14.refs_3_), channel_id=1, source_target_pairs={{0,32},{32,0},{64,96},{96,64},{128,160},{160,128},{192,224},{224,1... | collective-permute-start | bytes 786440 | tf_op jit(solution)/shard_map/ppermute | solution.py:24
  64.5 0.8 %collective-permute-done.17.refs_6_ = bf16[16,16,512]{2,1,0:T(8,128)(2,1)S(1)} collective-permute-done((bf16[16,16,512]{2,1,0:T(8,128)(2,1)S(1)}, bf16[16,16,512]{2,1,0:T(8,128)(2,1)S(1)}, u32[]{:S(2)}, u32[]{:S(2)}) %collective-permute-start.17) | collective-permute-done | bytes 262176 | tf_op jit(solution)/shard_map/ppermute | solution.py:24
  65.4 2.0 %collective-permute-start.18 = (bf16[16,16,512]{2,1,0:T(8,128)(2,1)S(1)}, bf16[16,16,512]{2,1,0:T(8,128)(2,1)S(1)}, u32[]{:S(2)}, u32[]{:S(2)}) collective-permute-start(bf16[16,16,512]{2,1,0:T(8,128)(2,1)S(1)} %collective-permute-done.17.refs_6_), channel_id=1, source_target_pairs={{0,32},{32,0},{64,96},{96,64},{128,160},{160,128},{192,224},{224,1... | collective-permute-start | bytes 786440 | tf_op jit(solution)/shard_map/ppermute | solution.py:24
  67.4 0.8 %collective-permute-done.11.refs_6_ = bf16[16,16,512]{2,1,0:T(8,128)(2,1)S(1)} collective-permute-done((bf16[16,16,512]{2,1,0:T(8,128)(2,1)S(1)}, bf16[16,16,512]{2,1,0:T(8,128)(2,1)S(1)}, u32[]{:S(2)}, u32[]{:S(2)}) %collective-permute-start.11) | collective-permute-done | bytes 262176 | tf_op jit(solution)/shard_map/ppermute | solution.py:24
  68.2 2.0 %collective-permute-start.12 = (bf16[16,16,512]{2,1,0:T(8,128)(2,1)S(1)}, bf16[16,16,512]{2,1,0:T(8,128)(2,1)S(1)}, u32[]{:S(2)}, u32[]{:S(2)}) collective-permute-start(bf16[16,16,512]{2,1,0:T(8,128)(2,1)S(1)} %collective-permute-done.11.refs_6_), channel_id=1, source_target_pairs={{0,32},{32,0},{64,96},{96,64},{128,160},{160,128},{192,224},{224,1... | collective-permute-start | bytes 786440 | tf_op jit(solution)/shard_map/ppermute | solution.py:24
  70.2 0.8 %collective-permute-done.8.refs_3_ = bf16[16,16,512]{2,1,0:T(8,128)(2,1)S(1)} collective-permute-done((bf16[16,16,512]{2,1,0:T(8,128)(2,1)S(1)}, bf16[16,16,512]{2,1,0:T(8,128)(2,1)S(1)}, u32[]{:S(2)}, u32[]{:S(2)}) %collective-permute-start.8) | collective-permute-done | bytes 262176 | tf_op jit(solution)/shard_map/ppermute | solution.py:24
  71.0 2.0 %collective-permute-start.10 = (bf16[16,16,512]{2,1,0:T(8,128)(2,1)S(1)}, bf16[16,16,512]{2,1,0:T(8,128)(2,1)S(1)}, u32[]{:S(2)}, u32[]{:S(2)}) collective-permute-start(bf16[16,16,512]{2,1,0:T(8,128)(2,1)S(1)} %collective-permute-done.8.refs_3_), channel_id=1, source_target_pairs={{0,32},{32,0},{64,96},{96,64},{128,160},{160,128},{192,224},{224,1... | collective-permute-start | bytes 786440 | tf_op jit(solution)/shard_map/ppermute | solution.py:24
  73.0 2.5 %update.2 = (f32[8,64,512]{2,1,0:T(8,128)}, f32[8,64,512]{2,1,0:T(8,128)}, bf16[8,64,512]{2,1,0:T(8,128)(2,1)}) custom-call(bf16[16,16,512]{2,1,0:T(8,128)(2,1)S(1)} %get-tuple-element.37.refs_0_, bf16[16,16,512]{2,1,0:T(8,128)(2,1)S(1)} %collective-permute-done.5.refs_1_, bf16[16,16,512]{2,1,0:T(8,128)(2,1)S(1)} %collective-permute-done.13.refs_2_, ...), custom_call_target="tpu_custom_call" | custom-call | flops 536870912 | bytes 8388608 | tf_op jit(solution)/shard_map/update/pallas_call | solution.py:148
  75.6 2.5 %update.3 = (f32[8,64,512]{2,1,0:T(8,128)}, f32[8,64,512]{2,1,0:T(8,128)}, bf16[8,64,512]{2,1,0:T(8,128)(2,1)}) custom-call(bf16[16,16,512]{2,1,0:T(8,128)(2,1)S(1)} %get-tuple-element.28.refs_0_, bf16[16,16,512]{2,1,0:T(8,128)(2,1)S(1)} %collective-permute-done.6.refs_1_, ...), custom_call_target="tpu_custom_call", output_to_operand_aliasing={{0}: (12, {}), {1}: (13, {}), {2}: (14, {})} | custom-call | flops 536870912 | bytes 8388608 | tf_op jit(solution)/shard_map/update/pallas_call | solution.py:148
  (34 shorter events, 3.0 us)
Async XLA Ops:
  0.6 1.6 %copy-start.4 = (bf16[1,128,8192]{2,1,0:T(8,128)(2,1)S(1)}, bf16[1,128,8192]{2,1,0:T(8,128)(2,1)}, u32[]{:S(2)}) copy-start(bf16[1,128,8192]{2,1,0:T(8,128)(2,1)} %param.6) | copy-start | bytes 6291460
  2.2 70.8 %copy-start = (bf16[1,1,8,512,512]{4,3,2,1,0:T(8,128)(2,1)S(1)}, bf16[1,1,8,512,512]{4,3,2,1,0:T(8,128)(2,1)}, u32[]{:S(2)}) copy-start(bf16[1,1,8,512,512]{4,3,2,1,0:T(8,128)(2,1)} %param.10) | copy-start | bytes 12582916
  2.2 70.8 %copy-start.1 = (f32[1,1,8,64,512]{4,3,2,1,0:T(8,128)S(1)}, f32[1,1,8,64,512]{4,3,2,1,0:T(8,128)}, u32[]{:S(2)}) copy-start(f32[1,1,8,64,512]{4,3,2,1,0:T(8,128)} %param.7) | copy-start | bytes 3145732
  2.2 70.8 %copy-start.2 = (f32[1,1,8,64,512]{4,3,2,1,0:T(8,128)S(1)}, f32[1,1,8,64,512]{4,3,2,1,0:T(8,128)}, u32[]{:S(2)}) copy-start(f32[1,1,8,64,512]{4,3,2,1,0:T(8,128)} %param.8) | copy-start | bytes 3145732
  2.2 70.8 %copy-start.3 = (bf16[1,1,8,64,512]{4,3,2,1,0:T(8,128)(2,1)S(1)}, bf16[1,1,8,64,512]{4,3,2,1,0:T(8,128)(2,1)}, u32[]{:S(2)}) copy-start(bf16[1,1,8,64,512]{4,3,2,1,0:T(8,128)(2,1)} %param.9) | copy-start | bytes 1572868
  2.5 4.9 %collective-permute-start = (bf16[2,16,8192]{2,1,0:T(8,128)(2,1)S(1)}, bf16[2,16,8192]{2,1,0:T(8,128)(2,1)S(1)}, u32[]{:S(2)}, u32[]{:S(2)}) collective-permute-start(bf16[2,16,8192]{2,1,0:T(8,128)(2,1)S(1)} %get-tuple-element.22), channel_id=1, source_target_pairs={{0,32},{32,0},{64,96},{96,64},{128,160},{160,128},{192,224},{224,1... | collective-permute-start | bytes 1572872 | tf_op jit(solution)/shard_map/ppermute | solution.py:24
  7.4 2.2 %collective-permute-start.1 = (bf16[2,16,8192]{2,1,0:T(8,128)(2,1)S(1)}, bf16[2,16,8192]{2,1,0:T(8,128)(2,1)S(1)}, u32[]{:S(2)}, u32[]{:S(2)}) collective-permute-start(bf16[2,16,8192]{2,1,0:T(8,128)(2,1)S(1)} %get-tuple-element.23), channel_id=1, source_target_pairs={{0,32},{32,0},{64,96},{96,64},{128,160},{160,128},{192,224},{224,1... | collective-permute-start | bytes 1572872 | tf_op jit(solution)/shard_map/ppermute | solution.py:24
  7.9 9.4 %collective-permute-start.2 = (bf16[16,8192]{1,0:T(8,128)(2,1)S(1)}, bf16[16,8192]{1,0:T(8,128)(2,1)S(1)}, u32[]{:S(2)}, u32[]{:S(2)}) collective-permute-start(bf16[16,8192]{1,0:T(8,128)(2,1)S(1)} %get-tuple-element.25), channel_id=1, source_target_pairs={{0,128},{32,160},{64,192},{96,224},{128,0},{160,32},{192,64},{224,... | collective-permute-start | bytes 786440 | tf_op jit(solution)/shard_map/ppermute | solution.py:24
  9.1 14.2 %collective-permute-start.3 = (bf16[16,8192]{1,0:T(8,128)(2,1)S(1)}, bf16[16,8192]{1,0:T(8,128)(2,1)S(1)}, u32[]{:S(2)}, u32[]{:S(2)}) collective-permute-start(bf16[16,8192]{1,0:T(8,128)(2,1)S(1)} %get-tuple-element.26), channel_id=1, source_target_pairs={{0,64},{32,96},{64,128},{96,160},{128,192},{160,224},{192,0},{224,... | collective-permute-start | bytes 786440 | tf_op jit(solution)/shard_map/ppermute | solution.py:24
  11.0 12.4 %collective-permute-start.4 = (bf16[16,8192]{1,0:T(8,128)(2,1)S(1)}, bf16[16,8192]{1,0:T(8,128)(2,1)S(1)}, u32[]{:S(2)}, u32[]{:S(2)}) collective-permute-start(bf16[16,8192]{1,0:T(8,128)(2,1)S(1)} %get-tuple-element.27), channel_id=1, source_target_pairs={{0,192},{32,224},{64,0},{96,32},{128,64},{160,96},{192,128},{224,1... | collective-permute-start | bytes 786440 | tf_op jit(solution)/shard_map/ppermute | solution.py:24
  47.2 6.4 %collective-permute-start.5 = (bf16[16,16,512]{2,1,0:T(8,128)(2,1)S(1)}, bf16[16,16,512]{2,1,0:T(8,128)(2,1)S(1)}, u32[]{:S(2)}, u32[]{:S(2)}) collective-permute-start(bf16[16,16,512]{2,1,0:T(8,128)(2,1)S(1)} %get-tuple-element.37.refs_0_), channel_id=1, source_target_pairs={{0,32},{32,0},{64,96},{96,64},{128,160},{160,128},{192,224},{224,1... | collective-permute-start | bytes 786440 | tf_op jit(solution)/shard_map/ppermute | solution.py:24
  51.2 5.7 %collective-permute-start.13 = (bf16[16,16,512]{2,1,0:T(8,128)(2,1)S(1)}, bf16[16,16,512]{2,1,0:T(8,128)(2,1)S(1)}, u32[]{:S(2)}, u32[]{:S(2)}) collective-permute-start(bf16[16,16,512]{2,1,0:T(8,128)(2,1)S(1)} %get-tuple-element.37.refs_0_), channel_id=1, source_target_pairs={{0,64},{32,224},{64,128},{96,32},{128,192},{160,96},{192,0},{224,1... | collective-permute-start | bytes 786440 | tf_op jit(solution)/shard_map/ppermute | solution.py:24
  53.6 3.3 %collective-permute-start.6 = (bf16[16,16,512]{2,1,0:T(8,128)(2,1)S(1)}, bf16[16,16,512]{2,1,0:T(8,128)(2,1)S(1)}, u32[]{:S(2)}, u32[]{:S(2)}) collective-permute-start(bf16[16,16,512]{2,1,0:T(8,128)(2,1)S(1)} %get-tuple-element.28.refs_0_), channel_id=1, source_target_pairs={{0,32},{32,0},{64,96},{96,64},{128,160},{160,128},{192,224},{224,1... | collective-permute-start | bytes 786440 | tf_op jit(solution)/shard_map/ppermute | solution.py:24
  53.6 6.4 %collective-permute-start.7 = (bf16[16,16,512]{2,1,0:T(8,128)(2,1)S(1)}, bf16[16,16,512]{2,1,0:T(8,128)(2,1)S(1)}, u32[]{:S(2)}, u32[]{:S(2)}) collective-permute-start(bf16[16,16,512]{2,1,0:T(8,128)(2,1)S(1)} %get-tuple-element.28.refs_0_), channel_id=1, source_target_pairs={{0,64},{32,224},{64,128},{96,32},{128,192},{160,96},{192,0},{224,1... | collective-permute-start | bytes 786440 | tf_op jit(solution)/shard_map/ppermute | solution.py:24
  55.1 7.7 %collective-permute-start.14 = (bf16[16,16,512]{2,1,0:T(8,128)(2,1)S(1)}, bf16[16,16,512]{2,1,0:T(8,128)(2,1)S(1)}, u32[]{:S(2)}, u32[]{:S(2)}) collective-permute-start(bf16[16,16,512]{2,1,0:T(8,128)(2,1)S(1)} %collective-permute-done.5.refs_1_), channel_id=1, source_target_pairs={{0,64},{32,224},{64,128},{96,32},{128,192},{160,96},{192,0},{224,1... | collective-permute-start | bytes 786440 | tf_op jit(solution)/shard_map/ppermute | solution.py:24
  56.9 8.4 %collective-permute-start.17 = (bf16[16,16,512]{2,1,0:T(8,128)(2,1)S(1)}, bf16[16,16,512]{2,1,0:T(8,128)(2,1)S(1)}, u32[]{:S(2)}, u32[]{:S(2)}) collective-permute-start(bf16[16,16,512]{2,1,0:T(8,128)(2,1)S(1)} %collective-permute-done.13.refs_2_), channel_id=1, source_target_pairs={{0,64},{32,224},{64,128},{96,32},{128,192},{160,96},{192,0},{224,1... | collective-permute-start | bytes 786440 | tf_op jit(solution)/shard_map/ppermute | solution.py:24
  60.1 7.3 %collective-permute-start.15 = (bf16[16,16,512]{2,1,0:T(8,128)(2,1)S(1)}, bf16[16,16,512]{2,1,0:T(8,128)(2,1)S(1)}, u32[]{:S(2)}, u32[]{:S(2)}) collective-permute-start(bf16[16,16,512]{2,1,0:T(8,128)(2,1)S(1)} %collective-permute-done.13.refs_2_), channel_id=1, source_target_pairs={{0,32},{32,0},{64,96},{96,64},{128,160},{160,128},{192,224},{224,1... | collective-permute-start | bytes 786440 | tf_op jit(solution)/shard_map/ppermute | solution.py:24
  60.1 8.1 %collective-permute-start.11 = (bf16[16,16,512]{2,1,0:T(8,128)(2,1)S(1)}, bf16[16,16,512]{2,1,0:T(8,128)(2,1)S(1)}, u32[]{:S(2)}, u32[]{:S(2)}) collective-permute-start(bf16[16,16,512]{2,1,0:T(8,128)(2,1)S(1)} %collective-permute-done.7.refs_2_), channel_id=1, source_target_pairs={{0,64},{32,224},{64,128},{96,32},{128,192},{160,96},{192,0},{224,1... | collective-permute-start | bytes 786440 | tf_op jit(solution)/shard_map/ppermute | solution.py:24
  62.9 8.1 %collective-permute-start.8 = (bf16[16,16,512]{2,1,0:T(8,128)(2,1)S(1)}, bf16[16,16,512]{2,1,0:T(8,128)(2,1)S(1)}, u32[]{:S(2)}, u32[]{:S(2)}) collective-permute-start(bf16[16,16,512]{2,1,0:T(8,128)(2,1)S(1)} %collective-permute-done.6.refs_1_), channel_id=1, source_target_pairs={{0,64},{32,224},{64,128},{96,32},{128,192},{160,96},{192,0},{224,1... | collective-permute-start | bytes 786440 | tf_op jit(solution)/shard_map/ppermute | solution.py:24
  62.9 10.1 %collective-permute-start.16 = (bf16[16,16,512]{2,1,0:T(8,128)(2,1)S(1)}, bf16[16,16,512]{2,1,0:T(8,128)(2,1)S(1)}, u32[]{:S(2)}, u32[]{:S(2)}) collective-permute-start(bf16[16,16,512]{2,1,0:T(8,128)(2,1)S(1)} %collective-permute-done.14.refs_3_), channel_id=1, source_target_pairs={{0,32},{32,0},{64,96},{96,64},{128,160},{160,128},{192,224},{224,1... | collective-permute-start | bytes 786440 | tf_op jit(solution)/shard_map/ppermute | solution.py:24
  65.4 7.6 %collective-permute-start.18 = (bf16[16,16,512]{2,1,0:T(8,128)(2,1)S(1)}, bf16[16,16,512]{2,1,0:T(8,128)(2,1)S(1)}, u32[]{:S(2)}, u32[]{:S(2)}) collective-permute-start(bf16[16,16,512]{2,1,0:T(8,128)(2,1)S(1)} %collective-permute-done.17.refs_6_), channel_id=1, source_target_pairs={{0,32},{32,0},{64,96},{96,64},{128,160},{160,128},{192,224},{224,1... | collective-permute-start | bytes 786440 | tf_op jit(solution)/shard_map/ppermute | solution.py:24
  67.4 8.2 %collective-permute-start.9 = (bf16[16,16,512]{2,1,0:T(8,128)(2,1)S(1)}, bf16[16,16,512]{2,1,0:T(8,128)(2,1)S(1)}, u32[]{:S(2)}, u32[]{:S(2)}) collective-permute-start(bf16[16,16,512]{2,1,0:T(8,128)(2,1)S(1)} %collective-permute-done.7.refs_2_), channel_id=1, source_target_pairs={{0,32},{32,0},{64,96},{96,64},{128,160},{160,128},{192,224},{224,1... | collective-permute-start | bytes 786440 | tf_op jit(solution)/shard_map/ppermute | solution.py:24
  68.2 7.4 %collective-permute-start.12 = (bf16[16,16,512]{2,1,0:T(8,128)(2,1)S(1)}, bf16[16,16,512]{2,1,0:T(8,128)(2,1)S(1)}, u32[]{:S(2)}, u32[]{:S(2)}) collective-permute-start(bf16[16,16,512]{2,1,0:T(8,128)(2,1)S(1)} %collective-permute-done.11.refs_6_), channel_id=1, source_target_pairs={{0,32},{32,0},{64,96},{96,64},{128,160},{160,128},{192,224},{224,1... | collective-permute-start | bytes 786440 | tf_op jit(solution)/shard_map/ppermute | solution.py:24
  71.0 4.6 %collective-permute-start.10 = (bf16[16,16,512]{2,1,0:T(8,128)(2,1)S(1)}, bf16[16,16,512]{2,1,0:T(8,128)(2,1)S(1)}, u32[]{:S(2)}, u32[]{:S(2)}) collective-permute-start(bf16[16,16,512]{2,1,0:T(8,128)(2,1)S(1)} %collective-permute-done.8.refs_3_), channel_id=1, source_target_pairs={{0,32},{32,0},{64,96},{96,64},{128,160},{160,128},{192,224},{224,1... | collective-permute-start | bytes 786440 | tf_op jit(solution)/shard_map/ppermute | solution.py:24
  (1 other events, 0.7 us)

commit v5 on v4

--- a/solution.py
+++ b/solution.py
@@ -59,19 +59,19 @@
 
 
 def pair_sum_kernel(groups, own, recv, *outs):
-    for n, k in enumerate(groups):
-        outs[n][...] = (own[k].astype(jnp.float32) + recv[n].astype(jnp.float32)).astype(own.dtype)
+    for out, (k, n) in zip(outs, groups):
+        out[...] = (own[k].astype(jnp.float32) + recv[n].astype(jnp.float32)).astype(own.dtype)
 
 
 def pair_sum(groups, own, recv, *extra):
     _, rows, cols = own.shape
     return pl.pallas_call(
-        lambda own, recv, *refs: pair_sum_kernel(groups, own, recv, *refs[-2:]),
+        lambda own, recv, *refs: pair_sum_kernel(groups, own, recv, *refs[-len(groups) :]),
         in_specs=[VMEM, VMEM] + [SMEM] * len(extra),
-        out_specs=[VMEM] * 2,
-        out_shape=[jax.ShapeDtypeStruct((rows, cols), own.dtype)] * 2,
+        out_specs=[VMEM] * len(groups),
+        out_shape=[jax.ShapeDtypeStruct((rows, cols), own.dtype)] * len(groups),
         compiler_params=pltpu.CompilerParams(vmem_limit_bytes=8 * MIB),
-        cost_estimate=pl.CostEstimate(flops=2 * rows * cols, bytes_accessed=2 * MIB, transcendentals=0),
+        cost_estimate=pl.CostEstimate(flops=len(groups) * rows * cols, bytes_accessed=len(groups) * MIB, transcendentals=0),
         name="pair_sum",
     )(own, recv, *extra)
 
@@ -192,9 +192,11 @@
 
     own, first, second = split(gradients.reshape(8, row_count // 8, col_count))
     first = cross(first)
-    to_far, to_next = pair_sum((2, 1), own, first)
+    to_far, to_next = pair_sum(((2, 0), (1, 1)), own, first)
     second, _ = tie(second, first)
-    to_prev, kept = pair_sum((3, 0), own, cross(second), owner_table)
+    second = cross(second)
+    (to_prev,) = pair_sum(((3, 0),), own, second)
+    (kept,) = pair_sum(((0, 1),), own, second, owner_table)
     parts = [kept, permute(to_far, y_shift(2)), permute(to_next, y_shift(1)), permute(to_prev, y_shift(-1))]
     (outgoing,) = place(owner_table, parts, owners, block)
     received = lax.all_to_all(outgoing, "fsdp", split_axis=0, concat_axis=0, tiled=True)

time: 78.4 us -> 78.4 us (level)
  no operation moved by 1% of the time
where the time goes in v5:
time: 78.4 us; the launch traced here: 78.3 us
  starting transfers between devices  29.8 us (38%)
  blocking collectives  23.1 us (29%)
  waiting for transfers between devices  16 us (20%)
  Pallas kernels  6.85 us (9%)
  local copies, waits for them, and re-layouts  1.64 us (2%)
  between operations  0.91 us (1%)
    ppermute x19, starting transfers between devices, permute(): return lax.ppermute(x, 'replica', pairs)  29.8 us
    all_to_all x1, blocking collectives, shards(): lax.all_to_all(outgoing, 'fsdp', split_axis=0, concat_axis=0, tiled=True)  23.1 us
    ppermute x19, waiting for transfers between devices, permute(): return lax.ppermute(x, 'replica', pairs)  16 us
    pallas_call x2, Pallas kernels, update(): pl.pallas_call(lambda *refs: update_kernel(first, *refs), in_specs=[VMEM]...  5.02 us
    unnamed x12, local copies, waits for them, and re-layouts  1.6 us
  transfers between devices with their start and end apart: 19, of which 7 were waited for; matrix products, arithmetic and copies ran while one was open for 0% of the time, Pallas kernels for 4%

profile of v5, /device:TPU:1, one launch (start us, length us, event | category | flops | bytes accessed | tf_op | source)
XLA Modules:
  0.0 78.3 jit_solution(1675922612753921171)
XLA Ops:
  0.6 1.6 %copy-done.4 = bf16[1,128,8192]{2,1,0:T(8,128)(2,1)S(1)} copy-done((bf16[1,128,8192]{2,1,0:T(8,128)(2,1)S(1)}, bf16[1,128,8192]{2,1,0:T(8,128)(2,1)}, u32[]{:S(2)}) %copy-start.4) | copy-done | bytes 2097176
  2.5 3.3 %collective-permute-start = (bf16[2,16,8192]{2,1,0:T(8,128)(2,1)S(1)}, bf16[2,16,8192]{2,1,0:T(8,128)(2,1)S(1)}, u32[]{:S(2)}, u32[]{:S(2)}) collective-permute-start(bf16[2,16,8192]{2,1,0:T(8,128)(2,1)S(1)} %get-tuple-element.20), channel_id=1, source_target_pairs={{0,32},{32,0},{64,96},{96,64},{128,160},{160,128},{192,224},{224,1... | collective-permute-start | bytes 1572872 | tf_op jit(solution)/shard_map/ppermute | solution.py:24
  5.8 1.5 %collective-permute-done.recv = bf16[2,16,8192]{2,1,0:T(8,128)(2,1)S(1)} collective-permute-done((bf16[2,16,8192]{2,1,0:T(8,128)(2,1)S(1)}, bf16[2,16,8192]{2,1,0:T(8,128)(2,1)S(1)}, u32[]{:S(2)}, u32[]{:S(2)}) %collective-permute-start) | collective-permute-done | bytes 524320 | tf_op jit(solution)/shard_map/ppermute | solution.py:24
  7.8 1.3 %collective-permute-start.2 = (bf16[16,8192]{1,0:T(8,128)(2,1)S(1)}, bf16[16,8192]{1,0:T(8,128)(2,1)S(1)}, u32[]{:S(2)}, u32[]{:S(2)}) collective-permute-start(bf16[16,8192]{1,0:T(8,128)(2,1)S(1)} %get-tuple-element.22), channel_id=1, source_target_pairs={{0,128},{32,160},{64,192},{96,224},{128,0},{160,32},{192,64},{224,... | collective-permute-start | bytes 786440 | tf_op jit(solution)/shard_map/ppermute | solution.py:24
  9.6 2.4 %collective-permute-start.4 = (bf16[16,8192]{1,0:T(8,128)(2,1)S(1)}, bf16[16,8192]{1,0:T(8,128)(2,1)S(1)}, u32[]{:S(2)}, u32[]{:S(2)}) collective-permute-start(bf16[16,8192]{1,0:T(8,128)(2,1)S(1)} %pair_sum.5), channel_id=1, source_target_pairs={{0,192},{32,224},{64,0},{96,32},{128,64},{160,96},{192,128},{224,1... | collective-permute-start | bytes 786440 | tf_op jit(solution)/shard_map/ppermute | solution.py:24
  12.6 4.6 %collective-permute-done.2.refs_1_ = bf16[16,8192]{1,0:T(8,128)(2,1)S(1)} collective-permute-done((bf16[16,8192]{1,0:T(8,128)(2,1)S(1)}, bf16[16,8192]{1,0:T(8,128)(2,1)S(1)}, u32[]{:S(2)}, u32[]{:S(2)}) %collective-permute-start.2) | collective-permute-done | bytes 262176 | tf_op jit(solution)/shard_map/ppermute | solution.py:24
  17.2 6.0 %collective-permute-done.3.refs_2_ = bf16[16,8192]{1,0:T(8,128)(2,1)S(1)} collective-permute-done((bf16[16,8192]{1,0:T(8,128)(2,1)S(1)}, bf16[16,8192]{1,0:T(8,128)(2,1)S(1)}, u32[]{:S(2)}, u32[]{:S(2)}) %collective-permute-start.3) | collective-permute-done | bytes 262176 | tf_op jit(solution)/shard_map/ppermute | solution.py:24
  23.3 0.8 place.1
  24.1 23.1 %all_to_all.5 = bf16[32,16,512]{2,1,0:T(8,128)(2,1)S(1)} all-to-all(bf16[32,16,512]{2,1,0:T(8,128)(2,1)S(1)} %place.1), channel_id=1, replica_groups=mesh['replica'=8,'fsdp'=32] {'fsdp'}, dimensions={0} | all-to-all | bytes 1048576 | tf_op jit(solution)/shard_map/all_to_all | solution.py:202
  47.2 4.1 %collective-permute-start.5 = (bf16[16,16,512]{2,1,0:T(8,128)(2,1)S(1)}, bf16[16,16,512]{2,1,0:T(8,128)(2,1)S(1)}, u32[]{:S(2)}, u32[]{:S(2)}) collective-permute-start(bf16[16,16,512]{2,1,0:T(8,128)(2,1)S(1)} %get-tuple-element.33.refs_0_), channel_id=1, source_target_pairs={{0,32},{32,0},{64,96},{96,64},{128,160},{160,128},{192,224},{224,1... | collective-permute-start | bytes 786440 | tf_op jit(solution)/shard_map/ppermute | solution.py:24
  51.3 2.3 %collective-permute-start.13 = (bf16[16,16,512]{2,1,0:T(8,128)(2,1)S(1)}, bf16[16,16,512]{2,1,0:T(8,128)(2,1)S(1)}, u32[]{:S(2)}, u32[]{:S(2)}) collective-permute-start(bf16[16,16,512]{2,1,0:T(8,128)(2,1)S(1)} %get-tuple-element.33.refs_0_), channel_id=1, source_target_pairs={{0,64},{32,224},{64,128},{96,32},{128,192},{160,96},{192,0},{224,1... | collective-permute-start | bytes 786440 | tf_op jit(solution)/shard_map/ppermute | solution.py:24
  53.6 1.5 %collective-permute-start.7 = (bf16[16,16,512]{2,1,0:T(8,128)(2,1)S(1)}, bf16[16,16,512]{2,1,0:T(8,128)(2,1)S(1)}, u32[]{:S(2)}, u32[]{:S(2)}) collective-permute-start(bf16[16,16,512]{2,1,0:T(8,128)(2,1)S(1)} %get-tuple-element.24.refs_0_), channel_id=1, source_target_pairs={{0,64},{32,224},{64,128},{96,32},{128,192},{160,96},{192,0},{224,1... | collective-permute-start | bytes 786440 | tf_op jit(solution)/shard_map/ppermute | solution.py:24
  55.4 1.5 %collective-permute-done.13.refs_2_ = bf16[16,16,512]{2,1,0:T(8,128)(2,1)S(1)} collective-permute-done((bf16[16,16,512]{2,1,0:T(8,128)(2,1)S(1)}, bf16[16,16,512]{2,1,0:T(8,128)(2,1)S(1)}, u32[]{:S(2)}, u32[]{:S(2)}) %collective-permute-start.13) | collective-permute-done | bytes 262176 | tf_op jit(solution)/shard_map/ppermute | solution.py:24
  56.9 3.1 %collective-permute-start.17 = (bf16[16,16,512]{2,1,0:T(8,128)(2,1)S(1)}, bf16[16,16,512]{2,1,0:T(8,128)(2,1)S(1)}, u32[]{:S(2)}, u32[]{:S(2)}) collective-permute-start(bf16[16,16,512]{2,1,0:T(8,128)(2,1)S(1)} %collective-permute-done.13.refs_2_), channel_id=1, source_target_pairs={{0,64},{32,224},{64,128},{96,32},{128,192},{160,96},{192,0},{224,1... | collective-permute-start | bytes 786440 | tf_op jit(solution)/shard_map/ppermute | solution.py:24
  60.0 2.8 %collective-permute-start.11 = (bf16[16,16,512]{2,1,0:T(8,128)(2,1)S(1)}, bf16[16,16,512]{2,1,0:T(8,128)(2,1)S(1)}, u32[]{:S(2)}, u32[]{:S(2)}) collective-permute-start(bf16[16,16,512]{2,1,0:T(8,128)(2,1)S(1)} %collective-permute-done.7.refs_2_), channel_id=1, source_target_pairs={{0,64},{32,224},{64,128},{96,32},{128,192},{160,96},{192,0},{224,1... | collective-permute-start | bytes 786440 | tf_op jit(solution)/shard_map/ppermute | solution.py:24
  62.9 1.7 %collective-permute-start.16 = (bf16[16,16,512]{2,1,0:T(8,128)(2,1)S(1)}, bf16[16,16,512]{2,1,0:T(8,128)(2,1)S(1)}, u32[]{:S(2)}, u32[]{:S(2)}) collective-permute-start(bf16[16,16,512]{2,1,0:T(8,128)(2,1)S(1)} %collective-permute-done.14.refs_3_), channel_id=1, source_target_pairs={{0,32},{32,0},{64,96},{96,64},{128,160},{160,128},{192,224},{224,1... | collective-permute-start | bytes 786440 | tf_op jit(solution)/shard_map/ppermute | solution.py:24
  64.6 0.8 collective-permute-done.17.refs_6_
  65.3 2.1 %collective-permute-start.18 = (bf16[16,16,512]{2,1,0:T(8,128)(2,1)S(1)}, bf16[16,16,512]{2,1,0:T(8,128)(2,1)S(1)}, u32[]{:S(2)}, u32[]{:S(2)}) collective-permute-start(bf16[16,16,512]{2,1,0:T(8,128)(2,1)S(1)} %collective-permute-done.17.refs_6_), channel_id=1, source_target_pairs={{0,32},{32,0},{64,96},{96,64},{128,160},{160,128},{192,224},{224,1... | collective-permute-start | bytes 786440 | tf_op jit(solution)/shard_map/ppermute | solution.py:24
  67.4 0.7 collective-permute-done.11.refs_6_
  68.2 2.1 %collective-permute-start.12 = (bf16[16,16,512]{2,1,0:T(8,128)(2,1)S(1)}, bf16[16,16,512]{2,1,0:T(8,128)(2,1)S(1)}, u32[]{:S(2)}, u32[]{:S(2)}) collective-permute-start(bf16[16,16,512]{2,1,0:T(8,128)(2,1)S(1)} %collective-permute-done.11.refs_6_), channel_id=1, source_target_pairs={{0,32},{32,0},{64,96},{96,64},{128,160},{160,128},{192,224},{224,1... | collective-permute-start | bytes 786440 | tf_op jit(solution)/shard_map/ppermute | solution.py:24
  70.2 0.8 collective-permute-done.8.refs_3_
  71.0 2.1 %collective-permute-start.10 = (bf16[16,16,512]{2,1,0:T(8,128)(2,1)S(1)}, bf16[16,16,512]{2,1,0:T(8,128)(2,1)S(1)}, u32[]{:S(2)}, u32[]{:S(2)}) collective-permute-start(bf16[16,16,512]{2,1,0:T(8,128)(2,1)S(1)} %collective-permute-done.8.refs_3_), channel_id=1, source_target_pairs={{0,32},{32,0},{64,96},{96,64},{128,160},{160,128},{192,224},{224,1... | collective-permute-start | bytes 786440 | tf_op jit(solution)/shard_map/ppermute | solution.py:24
  73.1 2.5 %update.2 = (f32[8,64,512]{2,1,0:T(8,128)}, f32[8,64,512]{2,1,0:T(8,128)}, bf16[8,64,512]{2,1,0:T(8,128)(2,1)}) custom-call(bf16[16,16,512]{2,1,0:T(8,128)(2,1)S(1)} %get-tuple-element.33.refs_0_, bf16[16,16,512]{2,1,0:T(8,128)(2,1)S(1)} %collective-permute-done.5.refs_1_, bf16[16,16,512]{2,1,0:T(8,128)(2,1)S(1)} %collective-permute-done.13.refs_2_, ...), custom_call_target="tpu_custom_call" | custom-call | flops 536870912 | bytes 8388608 | tf_op jit(solution)/shard_map/update/pallas_call | solution.py:148
  75.6 2.5 %update.3 = (f32[8,64,512]{2,1,0:T(8,128)}, f32[8,64,512]{2,1,0:T(8,128)}, bf16[8,64,512]{2,1,0:T(8,128)(2,1)}) custom-call(bf16[16,16,512]{2,1,0:T(8,128)(2,1)S(1)} %get-tuple-element.24.refs_0_, bf16[16,16,512]{2,1,0:T(8,128)(2,1)S(1)} %collective-permute-done.6.refs_1_, ...), custom_call_target="tpu_custom_call", output_to_operand_aliasing={{0}: (12, {}), {1}: (13, {}), {2}: (14, {})} | custom-call | flops 536870912 | bytes 8388608 | tf_op jit(solution)/shard_map/update/pallas_call | solution.py:148
  (35 shorter events, 2.3 us)
Async XLA Ops:
  2.2 9.7 %copy-start.5 = (s32[8,16]{1,0:T(8,128)S(1)}, s32[8,16]{1,0:T(8,128)}, u32[]{:S(2)}) copy-start(s32[8,16]{1,0:T(8,128)} %table.1) | copy-start | bytes 1540
  2.5 4.9 %collective-permute-start = (bf16[2,16,8192]{2,1,0:T(8,128)(2,1)S(1)}, bf16[2,16,8192]{2,1,0:T(8,128)(2,1)S(1)}, u32[]{:S(2)}, u32[]{:S(2)}) collective-permute-start(bf16[2,16,8192]{2,1,0:T(8,128)(2,1)S(1)} %get-tuple-element.20), channel_id=1, source_target_pairs={{0,32},{32,0},{64,96},{96,64},{128,160},{160,128},{192,224},{224,1... | collective-permute-start | bytes 1572872 | tf_op jit(solution)/shard_map/ppermute | solution.py:24
  7.3 2.2 %collective-permute-start.1 = (bf16[2,16,8192]{2,1,0:T(8,128)(2,1)S(1)}, bf16[2,16,8192]{2,1,0:T(8,128)(2,1)S(1)}, u32[]{:S(2)}, u32[]{:S(2)}) collective-permute-start(bf16[2,16,8192]{2,1,0:T(8,128)(2,1)S(1)} %get-tuple-element.21), channel_id=1, source_target_pairs={{0,32},{32,0},{64,96},{96,64},{128,160},{160,128},{192,224},{224,1... | collective-permute-start | bytes 1572872 | tf_op jit(solution)/shard_map/ppermute | solution.py:24
  7.7 65.3 %copy-start = (bf16[1,1,8,512,512]{4,3,2,1,0:T(8,128)(2,1)S(1)}, bf16[1,1,8,512,512]{4,3,2,1,0:T(8,128)(2,1)}, u32[]{:S(2)}) copy-start(bf16[1,1,8,512,512]{4,3,2,1,0:T(8,128)(2,1)} %param.10) | copy-start | bytes 12582916
  7.7 65.3 %copy-start.1 = (f32[1,1,8,64,512]{4,3,2,1,0:T(8,128)S(1)}, f32[1,1,8,64,512]{4,3,2,1,0:T(8,128)}, u32[]{:S(2)}) copy-start(f32[1,1,8,64,512]{4,3,2,1,0:T(8,128)} %param.7) | copy-start | bytes 3145732
  7.7 65.3 %copy-start.2 = (f32[1,1,8,64,512]{4,3,2,1,0:T(8,128)S(1)}, f32[1,1,8,64,512]{4,3,2,1,0:T(8,128)}, u32[]{:S(2)}) copy-start(f32[1,1,8,64,512]{4,3,2,1,0:T(8,128)} %param.8) | copy-start | bytes 3145732
  7.7 65.3 %copy-start.3 = (bf16[1,1,8,64,512]{4,3,2,1,0:T(8,128)(2,1)S(1)}, bf16[1,1,8,64,512]{4,3,2,1,0:T(8,128)(2,1)}, u32[]{:S(2)}) copy-start(bf16[1,1,8,64,512]{4,3,2,1,0:T(8,128)(2,1)} %param.9) | copy-start | bytes 1572868
  7.8 9.4 %collective-permute-start.2 = (bf16[16,8192]{1,0:T(8,128)(2,1)S(1)}, bf16[16,8192]{1,0:T(8,128)(2,1)S(1)}, u32[]{:S(2)}, u32[]{:S(2)}) collective-permute-start(bf16[16,8192]{1,0:T(8,128)(2,1)S(1)} %get-tuple-element.22), channel_id=1, source_target_pairs={{0,128},{32,160},{64,192},{96,224},{128,0},{160,32},{192,64},{224,... | collective-permute-start | bytes 786440 | tf_op jit(solution)/shard_map/ppermute | solution.py:24
  9.1 14.2 %collective-permute-start.3 = (bf16[16,8192]{1,0:T(8,128)(2,1)S(1)}, bf16[16,8192]{1,0:T(8,128)(2,1)S(1)}, u32[]{:S(2)}, u32[]{:S(2)}) collective-permute-start(bf16[16,8192]{1,0:T(8,128)(2,1)S(1)} %get-tuple-element.23), channel_id=1, source_target_pairs={{0,64},{32,96},{64,128},{96,160},{128,192},{160,224},{192,0},{224,... | collective-permute-start | bytes 786440 | tf_op jit(solution)/shard_map/ppermute | solution.py:24
  9.6 13.7 %collective-permute-start.4 = (bf16[16,8192]{1,0:T(8,128)(2,1)S(1)}, bf16[16,8192]{1,0:T(8,128)(2,1)S(1)}, u32[]{:S(2)}, u32[]{:S(2)}) collective-permute-start(bf16[16,8192]{1,0:T(8,128)(2,1)S(1)} %pair_sum.5), channel_id=1, source_target_pairs={{0,192},{32,224},{64,0},{96,32},{128,64},{160,96},{192,128},{224,1... | collective-permute-start | bytes 786440 | tf_op jit(solution)/shard_map/ppermute | solution.py:24
  47.2 6.4 %collective-permute-start.5 = (bf16[16,16,512]{2,1,0:T(8,128)(2,1)S(1)}, bf16[16,16,512]{2,1,0:T(8,128)(2,1)S(1)}, u32[]{:S(2)}, u32[]{:S(2)}) collective-permute-start(bf16[16,16,512]{2,1,0:T(8,128)(2,1)S(1)} %get-tuple-element.33.refs_0_), channel_id=1, source_target_pairs={{0,32},{32,0},{64,96},{96,64},{128,160},{160,128},{192,224},{224,1... | collective-permute-start | bytes 786440 | tf_op jit(solution)/shard_map/ppermute | solution.py:24
  51.3 5.6 %collective-permute-start.13 = (bf16[16,16,512]{2,1,0:T(8,128)(2,1)S(1)}, bf16[16,16,512]{2,1,0:T(8,128)(2,1)S(1)}, u32[]{:S(2)}, u32[]{:S(2)}) collective-permute-start(bf16[16,16,512]{2,1,0:T(8,128)(2,1)S(1)} %get-tuple-element.33.refs_0_), channel_id=1, source_target_pairs={{0,64},{32,224},{64,128},{96,32},{128,192},{160,96},{192,0},{224,1... | collective-permute-start | bytes 786440 | tf_op jit(solution)/shard_map/ppermute | solution.py:24
  53.6 3.3 %collective-permute-start.6 = (bf16[16,16,512]{2,1,0:T(8,128)(2,1)S(1)}, bf16[16,16,512]{2,1,0:T(8,128)(2,1)S(1)}, u32[]{:S(2)}, u32[]{:S(2)}) collective-permute-start(bf16[16,16,512]{2,1,0:T(8,128)(2,1)S(1)} %get-tuple-element.24.refs_0_), channel_id=1, source_target_pairs={{0,32},{32,0},{64,96},{96,64},{128,160},{160,128},{192,224},{224,1... | collective-permute-start | bytes 786440 | tf_op jit(solution)/shard_map/ppermute | solution.py:24
  53.6 6.4 %collective-permute-start.7 = (bf16[16,16,512]{2,1,0:T(8,128)(2,1)S(1)}, bf16[16,16,512]{2,1,0:T(8,128)(2,1)S(1)}, u32[]{:S(2)}, u32[]{:S(2)}) collective-permute-start(bf16[16,16,512]{2,1,0:T(8,128)(2,1)S(1)} %get-tuple-element.24.refs_0_), channel_id=1, source_target_pairs={{0,64},{32,224},{64,128},{96,32},{128,192},{160,96},{192,0},{224,1... | collective-permute-start | bytes 786440 | tf_op jit(solution)/shard_map/ppermute | solution.py:24
  55.1 7.7 %collective-permute-start.14 = (bf16[16,16,512]{2,1,0:T(8,128)(2,1)S(1)}, bf16[16,16,512]{2,1,0:T(8,128)(2,1)S(1)}, u32[]{:S(2)}, u32[]{:S(2)}) collective-permute-start(bf16[16,16,512]{2,1,0:T(8,128)(2,1)S(1)} %collective-permute-done.5.refs_1_), channel_id=1, source_target_pairs={{0,64},{32,224},{64,128},{96,32},{128,192},{160,96},{192,0},{224,1... | collective-permute-start | bytes 786440 | tf_op jit(solution)/shard_map/ppermute | solution.py:24
  56.9 8.4 %collective-permute-start.17 = (bf16[16,16,512]{2,1,0:T(8,128)(2,1)S(1)}, bf16[16,16,512]{2,1,0:T(8,128)(2,1)S(1)}, u32[]{:S(2)}, u32[]{:S(2)}) collective-permute-start(bf16[16,16,512]{2,1,0:T(8,128)(2,1)S(1)} %collective-permute-done.13.refs_2_), channel_id=1, source_target_pairs={{0,64},{32,224},{64,128},{96,32},{128,192},{160,96},{192,0},{224,1... | collective-permute-start | bytes 786440 | tf_op jit(solution)/shard_map/ppermute | solution.py:24
  60.0 7.4 %collective-permute-start.15 = (bf16[16,16,512]{2,1,0:T(8,128)(2,1)S(1)}, bf16[16,16,512]{2,1,0:T(8,128)(2,1)S(1)}, u32[]{:S(2)}, u32[]{:S(2)}) collective-permute-start(bf16[16,16,512]{2,1,0:T(8,128)(2,1)S(1)} %collective-permute-done.13.refs_2_), channel_id=1, source_target_pairs={{0,32},{32,0},{64,96},{96,64},{128,160},{160,128},{192,224},{224,1... | collective-permute-start | bytes 786440 | tf_op jit(solution)/shard_map/ppermute | solution.py:24
  60.0 8.1 %collective-permute-start.11 = (bf16[16,16,512]{2,1,0:T(8,128)(2,1)S(1)}, bf16[16,16,512]{2,1,0:T(8,128)(2,1)S(1)}, u32[]{:S(2)}, u32[]{:S(2)}) collective-permute-start(bf16[16,16,512]{2,1,0:T(8,128)(2,1)S(1)} %collective-permute-done.7.refs_2_), channel_id=1, source_target_pairs={{0,64},{32,224},{64,128},{96,32},{128,192},{160,96},{192,0},{224,1... | collective-permute-start | bytes 786440 | tf_op jit(solution)/shard_map/ppermute | solution.py:24
  62.8 8.1 %collective-permute-start.8 = (bf16[16,16,512]{2,1,0:T(8,128)(2,1)S(1)}, bf16[16,16,512]{2,1,0:T(8,128)(2,1)S(1)}, u32[]{:S(2)}, u32[]{:S(2)}) collective-permute-start(bf16[16,16,512]{2,1,0:T(8,128)(2,1)S(1)} %collective-permute-done.6.refs_1_), channel_id=1, source_target_pairs={{0,64},{32,224},{64,128},{96,32},{128,192},{160,96},{192,0},{224,1... | collective-permute-start | bytes 786440 | tf_op jit(solution)/shard_map/ppermute | solution.py:24
  62.9 10.1 %collective-permute-start.16 = (bf16[16,16,512]{2,1,0:T(8,128)(2,1)S(1)}, bf16[16,16,512]{2,1,0:T(8,128)(2,1)S(1)}, u32[]{:S(2)}, u32[]{:S(2)}) collective-permute-start(bf16[16,16,512]{2,1,0:T(8,128)(2,1)S(1)} %collective-permute-done.14.refs_3_), channel_id=1, source_target_pairs={{0,32},{32,0},{64,96},{96,64},{128,160},{160,128},{192,224},{224,1... | collective-permute-start | bytes 786440 | tf_op jit(solution)/shard_map/ppermute | solution.py:24
  65.3 7.7 %collective-permute-start.18 = (bf16[16,16,512]{2,1,0:T(8,128)(2,1)S(1)}, bf16[16,16,512]{2,1,0:T(8,128)(2,1)S(1)}, u32[]{:S(2)}, u32[]{:S(2)}) collective-permute-start(bf16[16,16,512]{2,1,0:T(8,128)(2,1)S(1)} %collective-permute-done.17.refs_6_), channel_id=1, source_target_pairs={{0,32},{32,0},{64,96},{96,64},{128,160},{160,128},{192,224},{224,1... | collective-permute-start | bytes 786440 | tf_op jit(solution)/shard_map/ppermute | solution.py:24
  67.4 8.2 %collective-permute-start.9 = (bf16[16,16,512]{2,1,0:T(8,128)(2,1)S(1)}, bf16[16,16,512]{2,1,0:T(8,128)(2,1)S(1)}, u32[]{:S(2)}, u32[]{:S(2)}) collective-permute-start(bf16[16,16,512]{2,1,0:T(8,128)(2,1)S(1)} %collective-permute-done.7.refs_2_), channel_id=1, source_target_pairs={{0,32},{32,0},{64,96},{96,64},{128,160},{160,128},{192,224},{224,1... | collective-permute-start | bytes 786440 | tf_op jit(solution)/shard_map/ppermute | solution.py:24
  68.2 7.4 %collective-permute-start.12 = (bf16[16,16,512]{2,1,0:T(8,128)(2,1)S(1)}, bf16[16,16,512]{2,1,0:T(8,128)(2,1)S(1)}, u32[]{:S(2)}, u32[]{:S(2)}) collective-permute-start(bf16[16,16,512]{2,1,0:T(8,128)(2,1)S(1)} %collective-permute-done.11.refs_6_), channel_id=1, source_target_pairs={{0,32},{32,0},{64,96},{96,64},{128,160},{160,128},{192,224},{224,1... | collective-permute-start | bytes 786440 | tf_op jit(solution)/shard_map/ppermute | solution.py:24
  71.0 4.6 %collective-permute-start.10 = (bf16[16,16,512]{2,1,0:T(8,128)(2,1)S(1)}, bf16[16,16,512]{2,1,0:T(8,128)(2,1)S(1)}, u32[]{:S(2)}, u32[]{:S(2)}) collective-permute-start(bf16[16,16,512]{2,1,0:T(8,128)(2,1)S(1)} %collective-permute-done.8.refs_3_), channel_id=1, source_target_pairs={{0,32},{32,0},{64,96},{96,64},{128,160},{160,128},{192,224},{224,1... | collective-permute-start | bytes 786440 | tf_op jit(solution)/shard_map/ppermute | solution.py:24
  (1 other events, 1.6 us)
